TPU v7x, 128 devices: a whole 4x4x4 slice. The times are simulated.
128 devices in a mesh: rows: 32 (over z, y, core), mem: 4 (over x).
Axes of the slice: x: 4, y: 4, z: 4, core: 2. Of those that a mesh axis runs over, the one named last changes fastest.
Arguments:
- fine_members: float32 [16, 8, 512, 512], P('mem', None, 'rows'), may hold values from -6 to 6
- coarse_members: float32 [32, 8, 256, 256], P('mem', None, 'rows'), may hold values from -6 to 6
- diffusion: float32 [8], replicated, may hold values from 0.02 to 0.08
- hyper: float32 [8], replicated, may hold values from 0.002 to 0.008
- drift: float32 [8], replicated, may hold values from -0.2 to 0.2
- obs_value: float32 [32768], P('rows'), may hold values from -6 to 6
- obs_var: float32 [32768], P('rows'), may hold values from 0.5 to 5
- obs_row: int32 [32768], P('rows'), may hold values from 0 to 511, as said below
- obs_col: int32 [32768], P('rows'), may hold values from 0 to 511
- obs_layer: int32 [32768], P('rows'), may hold values from 0 to 7
- obs_count: int32 [32], P('rows'), may hold values from 256 to 1024, as said below
Outputs:
- analysis_mean: float32 [8, 512, 512], P(None, 'rows')
- pair_update: float32 [16, 8, 512, 512], P('mem', None, 'rows')
Inputs may be any that keep to these rules, and one draw needn't show every extreme that they name: `obs_row`: observation slot s belongs to row tile t = s // 1024, and its row lies in that tile: from t * 16 to t * 16 + 15. `obs_count`: some tile has all 1024 slots live in every draw.
All inputs are finite; a program needn't handle non-finite values.
Results may differ from a plain program's by a relative error of at most 0.00016.
Values sent between devices are 32-bit elements; how exact they have to be, the bound alone decides.
A program may use at most 128 MiB of HBM per device.

v0:
```python
import math

import jax
import jax.numpy as jnp
from jax import lax
from jax.sharding import PartitionSpec as P

STEPS = 3


def extended(cells, sides, width):
    for axis, dim in sides:
        count = lax.axis_size(axis)
        ends = count - 1
        head = lax.slice_in_dim(cells, 0, width, axis=dim)
        tail = lax.slice_in_dim(cells, cells.shape[dim] - width, cells.shape[dim], axis=dim)
        cells = jnp.concatenate(
            [
                lax.ppermute(tail, axis, [(i, (i + 1) % count) for i in range(ends)]),
                cells,
                lax.ppermute(head, axis, [((i + 1) % count, i) for i in range(ends)]),
            ],
            axis=dim,
        )
    return cells


def restrict(fine):
    shape = fine.shape
    blocks = fine.reshape(shape[:-2] + (shape[-2] // 2, 2, shape[-1] // 2, 2))
    return blocks.mean(axis=(-3, -1))


def prolong(coarse):
    return jnp.repeat(jnp.repeat(coarse, 2, axis=-2), 2, axis=-1)


def advance(padded, first_row, grid_rows, diffusion, hyper, drift):
    count = padded.shape[2]
    rows_at = first_row + jnp.arange(count, dtype=jnp.int32)
    inside = ((rows_at >= 0) & (rows_at < grid_rows)).astype(padded.dtype)[:, None]

    def plane(field):
        core = field[:, :, 1:-1]
        return (
            field[:, :, 2:]
            + field[:, :, :-2]
            + jnp.roll(core, 1, axis=3)
            + jnp.roll(core, -1, axis=3)
            - 4.0 * core
        )

    first = plane(padded) * inside[1:-1]
    second = plane(first)
    centre = padded[:, :, 2:-2]
    side = jnp.roll(centre, -1, axis=3) - jnp.roll(centre, 1, axis=3)
    upper = jnp.pad(centre[:, 1:], ((0, 0), (0, 1), (0, 0), (0, 0)))
    lower = jnp.pad(centre[:, :-1], ((0, 0), (1, 0), (0, 0), (0, 0)))
    out = (
        centre
        + diffusion[None, :, None, None] * first[:, :, 1:-1]
        - hyper[None, :, None, None] * second
        - 0.5 * drift[None, :, None, None] * side
        + 0.1 * (upper - 2.0 * centre + lower)
    )
    return out * inside[2:-2]


def contract(weights, fields):
    return jnp.einsum("em,ekrc->mkrc", weights, fields, precision=lax.Precision.HIGHEST)


def per_device(
    fine_members,
    coarse_members,
    diffusion,
    hyper,
    drift,
    obs_value,
    obs_var,
    obs_row,
    obs_col,
    obs_layer,
    obs_count,
):
    tile = lax.axis_index("rows")
    tiles = lax.axis_size("rows")
    groups = lax.axis_size("mem")
    member = lax.axis_index("mem")
    level_dev = coarse_members.shape[0]
    pairs_dev = fine_members.shape[0]
    rows_f = fine_members.shape[2]
    rows_c = coarse_members.shape[2]
    cols_f = fine_members.shape[3]
    cols_c = coarse_members.shape[3]
    level_all = level_dev * groups
    pairs_all = pairs_dev * groups
    fine = fine_members
    members_c = jnp.concatenate([coarse_members, restrict(fine_members)], 0)
    soft_c = (diffusion * 0.25, hyper * 0.0625, drift * 0.5)
    for step in range(STEPS):
        fine_pad = extended(fine, (("rows", 2),), 2)
        coarse_pad = extended(members_c, (("rows", 2),), 2)
        fine = advance(fine_pad, tile * rows_f - 2, tiles * rows_f, diffusion, hyper, drift)
        members_c = advance(
            coarse_pad, tile * rows_c - 2, tiles * rows_c, soft_c[0], soft_c[1], soft_c[2]
        )
    level_c = members_c[:level_dev]
    pair_c = members_c[level_dev:]
    sums = lax.psum((jnp.sum(fine, 0), jnp.sum(pair_c, 0), jnp.sum(level_c, 0)), "mem")
    mean_f = sums[0] / pairs_all
    mean_p = sums[1] / pairs_all
    mean_l = sums[2] / level_all
    level_anom = (level_c - mean_l) / math.sqrt(level_all - 1)
    fine_anom = fine - mean_f
    pair_anom = pair_c - mean_p
    local_row = obs_row - tile * rows_f
    fine_index = (obs_layer * rows_f + local_row) * cols_f + obs_col
    coarse_index = (obs_layer * rows_c + local_row // 2) * cols_c + obs_col // 2
    level_obs = jnp.take(level_anom.reshape(level_dev, -1), coarse_index, axis=1)
    pair_obs = (
        jnp.take(fine_anom.reshape(pairs_dev, -1), fine_index, axis=1)
        - jnp.take(pair_anom.reshape(pairs_dev, -1), coarse_index, axis=1)
    ) / math.sqrt(pairs_all - 1)
    level_all_obs, pair_all_obs = (
        lax.all_gather(level_obs, "mem", axis=0, tiled=True),
        lax.all_gather(pair_obs, "mem", axis=0, tiled=True),
    )
    columns = jnp.concatenate([level_all_obs, pair_all_obs], 0)
    mean_obs = (
        jnp.take(mean_l.reshape(-1), coarse_index)
        + jnp.take(mean_f.reshape(-1), fine_index)
        - jnp.take(mean_p.reshape(-1), coarse_index)
    )
    innov = obs_value - mean_obs
    live = jnp.arange(obs_value.shape[0], dtype=jnp.int32) < obs_count[0]
    weight = jnp.where(live, 1.0 / obs_var, 0.0)
    gram_part = jnp.dot(columns * weight[None, :], columns.T, precision=lax.Precision.HIGHEST)
    rhs_part = jnp.dot(columns, weight * innov, precision=lax.Precision.HIGHEST)
    gram, rhs = lax.psum((gram_part, rhs_part), "rows")
    total = level_all + pairs_all
    system = jnp.eye(total, dtype=jnp.float32) + gram
    factor = jnp.linalg.cholesky(system)
    solved = jax.scipy.linalg.cho_solve((factor, True), jnp.concatenate([rhs[:, None], gram], 1))
    coef = jnp.concatenate([solved[:, :1], -0.5 * solved[:, 1 + level_all :]], 1)
    pair_cols = (fine_anom - prolong(pair_anom)) / math.sqrt(pairs_all - 1)
    mu = prolong(mean_l) + mean_f - prolong(mean_p)
    owned = lax.dynamic_slice(coef, (0, 1 + member * pairs_dev), (total, pairs_dev))
    chosen = jnp.concatenate([coef[:, :1], owned], 1)
    coarse_init = jnp.zeros((1 + pairs_dev,) + level_anom.shape[1:], jnp.float32)
    fine_init = jnp.zeros((1 + pairs_dev,) + pair_cols.shape[1:], jnp.float32)
    piece = lax.all_gather(level_anom, "mem", axis=0, tiled=True)
    weights = lax.slice_in_dim(chosen, 0, piece.shape[0], axis=0)
    coarse_incr = coarse_init + contract(weights, piece)
    piece = lax.all_gather(pair_cols, "mem", axis=0, tiled=True)
    weights = lax.dynamic_slice_in_dim(chosen, level_all, piece.shape[0], 0)
    fine_incr = fine_init + contract(weights, piece)
    incr = prolong(coarse_incr) + fine_incr
    mean_incr = incr[0]
    pair_incr = incr[1:]
    analysis_mean = mu + mean_incr
    pair_update = math.sqrt(pairs_all - 1) * (pair_cols + pair_incr)
    return (analysis_mean, pair_update)


def solution(mesh):
    in_specs = (
        P("mem", None, "rows", None),
        P("mem", None, "rows", None),
        P(),
        P(),
        P(),
        P("rows"),
        P("rows"),
        P("rows"),
        P("rows"),
        P("rows"),
        P("rows"),
    )
    out_specs = (P(None, "rows", None), P("mem", None, "rows", None))
    return jax.shard_map(
        per_device, mesh=mesh, in_specs=in_specs, out_specs=out_specs, check_vma=False
    )
```

profile of v0, /device:TPU:0, one launch (start us, length us, event | category | flops | bytes accessed | tf_op | source)
XLA Modules:
  0.0 493.0 jit_solution(1095336677089485694)
XLA Ops:
  7.2 2.0 copy.154
  12.5 8.7 %copy.143 = f32[4,8,16,512]{1,3,2,0:T(8,128)} copy(f32[4,8,16,512]{3,2,1,0:T(8,128)S(1)} %copy-done) | data formatting | bytes 2097152 | tf_op args[0]
  21.3 17.7 %reduce_sum.36 = f32[4,8,8,256]{1,3,2,0:T(8,128)} reduce(f32[4,8,8,2,256,2]{1,5,4,3,2,0:T(2,128)} %bitcast.65, f32[]{:T(128)} %constant.175.clone.1), dimensions={3,5}, to_apply=%region_0.0 | reduce | flops 196608 | bytes 1310724 | tf_op jit(solution)/shard_map/reduce_sum | solution.py:31
  38.9 2.8 copy.144
  45.5 6.3 %collective-permute-start.1 = (f32[12,8,2,256]{3,0,2,1:T(8,128)}, f32[12,8,2,256]{3,0,2,1:T(8,128)}, u32[]{:S(2)}, u32[]{:S(2)}) collective-permute-start(f32[12,8,2,256]{3,0,2,1:T(8,128)} %get-tuple-element.124), channel_id=1, source_target_pairs={{0,4},{4,8},{8,12},{12,16},{16,20},{20,24},{24,28},{28,32},{32,36}... | collective-permute-start | bytes 589832 | tf_op jit(solution)/shard_map/ppermute | solution.py:19
  51.9 1.9 fusion.148
  53.8 1.7 fusion.150
  56.4 1.7 fusion.161
  58.1 1.5 fusion.159
  64.3 1.9 fusion.22
  68.7 3.0 fusion.81
  74.0 3.8 collective-permute-start.9
  79.9 1.8 fusion.10
  84.2 1.4 fusion.74
  87.8 4.3 collective-permute-start.3
  93.5 1.8 fusion.20
  96.1 2.8 fusion.82
  101.3 4.5 collective-permute-start.11
  107.9 1.8 fusion.18
  110.5 4.7 fusion.113
  117.6 1.4 fusion.66
  121.0 5.6 %collective-permute-start.5 = (f32[12,8,2,256]{3,0,2,1:T(8,128)S(1)}, f32[12,8,2,256]{3,0,2,1:T(8,128)S(1)}, u32[]{:S(2)}, u32[]{:S(2)}) collective-permute-start(f32[12,8,2,256]{3,0,2,1:T(8,128)S(1)} %get-tuple-element.108), channel_id=1, source_target_pairs={{0,4},{4,8},{8,12},{12,16},{16,20},{20,24},{24,28},{28,32},{32,36}... | collective-permute-start | bytes 589832 | tf_op jit(solution)/shard_map/ppermute | solution.py:19
  129.8 1.4 fusion.58
  132.8 60.2 %all-reduce.16.cloned.1.call-done = (f32[8,8,256]{2,1,0:T(8,128)}, f32[8,8,256]{2,1,0:T(8,128)}, f32[8,16,512]{2,1,0:T(8,128)}) async-done(((f32[8,8,256]{2,1,0:T(8,128)}, f32[8,8,256]{2,1,0:T(8,128)}, f32[8,16,512]{2,1,0:T(8,128)}), (f32[8,8,256]{2,1,0:T(8,128)}, f32[8,8,256]{2,1,0:T(8,128)}, f32[8,16,512]{2,1,0:T(8,128)})) %all-reduce.16.cloned.1.call-update) | async-done | bytes 393232 | tf_op jit(solution)/shard_map/psum | solution.py:110
  193.0 1.5 fusion.111
  197.1 2.8 copy.178
  199.9 6.1 %broadcast_in_dim.134 = f32[4,8,16,256,2]{2,1,4,3,0:T(8,128)} broadcast(f32[4,8,16,256]{2,1,3,0:T(8,128)} %copy.178), dimensions={0,1,2,3} | broadcast | bytes 1572864 | tf_op jit(solution)/shard_map/broadcast_in_dim | solution.py:35
  205.9 5.4 %copy.179 = f32[4,8,16,512]{3,0,2,1:T(4,128)S(1)} copy(f32[4,8,16,512]{2,1,3,0:T(8,128)} %bitcast.67) | data formatting | bytes 2097152 | tf_op jit(solution)/shard_map/reshape | solution.py:35
  211.4 1.9 subtract_multiply_fusion
  216.1 15.9 %copy.168 = f32[4,65536]{0,1:T(8,128)} copy(f32[4,65536]{1,0:T(4,128)S(1)} %bitcast.71) | data formatting | bytes 2097152 | tf_op jit(solution)/shard_map/reshape | solution.py:122
  232.0 5.1 %copy.169 = f32[4,16384]{0,1:T(8,128)} copy(f32[4,16384]{1,0:T(4,128)S(1)} %bitcast.73) | data formatting | bytes 524288 | tf_op jit(solution)/shard_map/reshape | solution.py:123
  237.1 14.4 %gather_fusion.1 = f32[1024,4]{1,0:T(8,128)S(1)} fusion(f32[4,65536]{0,1:T(8,128)} %copy.168, s32[1024]{0:T(1024)S(1)} %get-tuple-element.24), kind=kCustom, calls=%fused_computation.3 | custom fusion | bytes 36864 | tf_op jit(solution)/shard_map/jit(_take)/gather | solution.py:122
  251.6 6.2 %gather_fusion.3 = f32[1024]{0:T(1024)S(1)} fusion(f32[65536]{0:T(1024)S(1)} %bitcast.64, s32[1024]{0:T(1024)S(1)} %get-tuple-element.24), kind=kCustom, calls=%fused_computation.5 | custom fusion | bytes 12288 | tf_op jit(solution)/shard_map/jit(_take)/gather | solution.py:132
  257.8 6.3 %gather_fusion.2 = f32[1024,4]{1,0:T(8,128)S(1)} fusion(f32[4,16384]{0,1:T(8,128)} %copy.169, s32[1024]{0:T(1024)S(1)} %get-tuple-element.130), kind=kCustom, calls=%fused_computation.4 | custom fusion | bytes 36864 | tf_op jit(solution)/shard_map/jit(_take)/gather | solution.py:123
  264.1 6.2 %gather_fusion.4 = f32[1024]{0:T(1024)S(1)} fusion(f32[16384]{0:T(1024)S(1)} %bitcast.62, s32[1024]{0:T(1024)S(1)} %get-tuple-element.130), kind=kCustom, calls=%fused_computation.clone | custom fusion | bytes 12288 | tf_op jit(solution)/shard_map/jit(_take)/gather | solution.py:131
  270.3 6.2 %gather_fusion.5 = f32[1024]{0:T(1024)S(1)} fusion(f32[16384]{0:T(1024)S(1)} %bitcast.63, s32[1024]{0:T(1024)S(1)} %get-tuple-element.130), kind=kCustom, calls=%fused_computation.1.clone | custom fusion | bytes 12288 | tf_op jit(solution)/shard_map/jit(_take)/gather | solution.py:133
  277.1 11.9 %all-gather = f32[4,4,1024]{2,1,0:T(4,128)S(1)} all-gather(f32[1,4,1024]{2,1,0:T(4,128)S(1)} %copy.170), channel_id=1, replica_groups=mesh['rows'=32,'mem'=4] {'mem'}, dimensions={0}, use_global_device_ids=true | all-gather | bytes 81920 | tf_op jit(solution)/shard_map/all_gather | solution.py:127
  289.0 5.3 %copy.166 = f32[8,16384]{0,1:T(8,128)} copy(f32[8,16384]{1,0:T(8,128)S(1)} %bitcast.70) | data formatting | bytes 1048576 | tf_op jit(solution)/shard_map/reshape | solution.py:120
  294.3 6.2 %gather_fusion = f32[1024,8]{1,0:T(8,128)S(1)} fusion(f32[8,16384]{0,1:T(8,128)} %copy.166, s32[1024]{0:T(1024)S(1)} %get-tuple-element.130), kind=kCustom, calls=%fused_computation.2 | custom fusion | bytes 69632 | tf_op jit(solution)/shard_map/jit(_take)/gather | solution.py:120
  300.9 12.0 %all_gather.12 = f32[32,1024]{1,0:T(8,128)S(1)} all-gather(f32[8,1024]{1,0:T(8,128)S(1)} %copy.167), channel_id=1, replica_groups=mesh['rows'=32,'mem'=4] {'mem'}, dimensions={0}, use_global_device_ids=true | all-gather | bytes 163840 | tf_op jit(solution)/shard_map/all_gather | solution.py:126
  313.5 124.2 %all-reduce.12 = (f32[48,48]{1,0:T(8,128)S(1)}, f32[48,1]{1,0:T(8,128)S(1)}) all-reduce(f32[48,48]{1,0:T(8,128)S(1)} %fusion.84, f32[48,1]{1,0:T(8,128)S(1)} %convolution_bitcast_fusion), channel_id=1, replica_groups=mesh['rows'=32,'mem'=4] {'rows'}, use_global_device_ids=true, to_apply=%region_7.8 | all-reduce | flops 2352 | bytes 18816 | tf_op jit(solution)/shard_map/psum | solution.py:140
  437.8 4.4 cholesky.17
  443.5 3.7 custom-call.10
  455.5 2.7 fusion.102
  458.4 3.1 copy.176
  461.5 7.2 %broadcast_in_dim.132 = f32[5,8,16,256,2]{2,1,4,3,0:T(8,128)} broadcast(f32[5,8,16,256]{2,1,3,0:T(8,128)} %copy.176), dimensions={0,1,2,3} | broadcast | bytes 1966080 | tf_op jit(solution)/shard_map/broadcast_in_dim | solution.py:35
  468.7 7.1 %copy.182 = f32[5,8,16,512]{3,0,2,1:T(8,128)S(1)} copy(f32[5,8,16,512]{2,1,3,0:T(8,128)} %bitcast.66) | data formatting | bytes 2621440 | tf_op jit(solution)/shard_map/reshape | solution.py:35
  475.8 7.0 %fusion.2 = f32[5,8,16,512]{3,0,2,1:T(8,128)S(1)} fusion(f32[5,8,16,512]{3,0,2,1:T(8,128)S(1)} %copy.182, f32[16,8,16,512]{3,2,1,0:T(8,128)} %all-gather.6.cloned.1.call-done, f32[48,5]{0,1:T(8,128)S(1)} %pad_maximum_fusion.5), kind=kOutput, calls=%fused_computation.8 | convolution fusion | flops 63242240 | bytes 6816704 | tf_op jit(solution)/shard_map/em,ekrc->mkrc/dot_general | solution.py:70
  (211 shorter events, 60.1 us)
Async XLA Ops:
  7.2 5.4 %copy-start = (f32[4,8,16,512]{3,2,1,0:T(8,128)S(1)}, f32[4,8,16,512]{3,2,1,0:T(8,128)}, u32[]{:S(2)}) copy-start(f32[4,8,16,512]{3,2,1,0:T(8,128)} %param.13) | copy-start | bytes 3145732
  7.2 185.8 %all-reduce.16.cloned.1.call-start = ((), (), s32[]{:S(2)}) async-start(), calls=%async_computation.2 | async-start | bytes 786432 | tf_op jit(solution)/shard_map/psum | solution.py:110
  9.9 51.7 %collective-permute-start.7 = (f32[4,8,2,512]{3,0,2,1:T(4,128)}, f32[4,8,2,512]{3,0,2,1:T(4,128)S(1)}, u32[]{:S(2)}, u32[]{:S(2)}) collective-permute-start(f32[4,8,2,512]{3,0,2,1:T(4,128)} %get-tuple-element.95), channel_id=1, source_target_pairs={{0,4},{4,8},{8,12},{12,16},{16,20},{20,24},{24,28},{28,32},{32,36}... | collective-permute-start | bytes 393224 | tf_op jit(solution)/shard_map/ppermute | solution.py:19
  11.2 51.2 %collective-permute-start.6 = (f32[4,8,2,512]{3,0,2,1:T(4,128)}, f32[4,8,2,512]{3,0,2,1:T(4,128)}, u32[]{:S(2)}, u32[]{:S(2)}) collective-permute-start(f32[4,8,2,512]{3,0,2,1:T(4,128)} %get-tuple-element.94), channel_id=1, source_target_pairs={{4,0},{8,4},{12,8},{16,12},{20,16},{24,20},{28,24},{32,28},{36,32}... | collective-permute-start | bytes 393224 | tf_op jit(solution)/shard_map/ppermute | solution.py:21
  44.2 33.8 %collective-permute-start = (f32[12,8,2,256]{3,0,2,1:T(8,128)}, f32[12,8,2,256]{3,0,2,1:T(8,128)S(1)}, u32[]{:S(2)}, u32[]{:S(2)}) collective-permute-start(f32[12,8,2,256]{3,0,2,1:T(8,128)} %get-tuple-element.125), channel_id=1, source_target_pairs={{4,0},{8,4},{12,8},{16,12},{20,16},{24,20},{28,24},{32,28},{36,32}... | collective-permute-start | bytes 589832 | tf_op jit(solution)/shard_map/ppermute | solution.py:21
  45.5 32.5 %collective-permute-start.1 = (f32[12,8,2,256]{3,0,2,1:T(8,128)}, f32[12,8,2,256]{3,0,2,1:T(8,128)}, u32[]{:S(2)}, u32[]{:S(2)}) collective-permute-start(f32[12,8,2,256]{3,0,2,1:T(8,128)} %get-tuple-element.124), channel_id=1, source_target_pairs={{0,4},{4,8},{8,12},{12,16},{16,20},{20,24},{24,28},{28,32},{32,36}... | collective-permute-start | bytes 589832 | tf_op jit(solution)/shard_map/ppermute | solution.py:19
  59.6 1.4 copy-start.26
  59.6 1.4 copy-start.27
  66.2 1.2 copy-start.4
  66.2 1.5 copy-start.7
  66.3 1.8 copy-start.8
  66.3 1.8 copy-start.20
  66.3 1.9 copy-start.21
  66.9 1.7 copy-start.3
  72.7 19.4 %collective-permute-start.8 = (f32[4,8,2,512]{3,0,2,1:T(4,128)S(1)}, f32[4,8,2,512]{3,0,2,1:T(4,128)S(1)}, u32[]{:S(2)}, u32[]{:S(2)}) collective-permute-start(f32[4,8,2,512]{3,0,2,1:T(4,128)S(1)} %get-tuple-element.87), channel_id=1, source_target_pairs={{4,0},{8,4},{12,8},{16,12},{20,16},{24,20},{28,24},{32,28},{36,32}... | collective-permute-start | bytes 393224 | tf_op jit(solution)/shard_map/ppermute | solution.py:21
  74.0 18.1 %collective-permute-start.9 = (f32[4,8,2,512]{3,0,2,1:T(4,128)S(1)}, f32[4,8,2,512]{3,0,2,1:T(4,128)S(1)}, u32[]{:S(2)}, u32[]{:S(2)}) collective-permute-start(f32[4,8,2,512]{3,0,2,1:T(4,128)S(1)} %get-tuple-element.86), channel_id=1, source_target_pairs={{0,4},{4,8},{8,12},{12,16},{16,20},{20,24},{24,28},{28,32},{32,36}... | collective-permute-start | bytes 393224 | tf_op jit(solution)/shard_map/ppermute | solution.py:19
  81.7 1.2 copy-start.9
  81.7 1.4 copy-start.10
  81.7 1.6 copy-start.15
  81.7 1.7 copy-start.16
  82.1 1.8 copy-start.5
  82.1 2.1 copy-start.6
  86.5 28.7 %collective-permute-start.2 = (f32[12,8,2,256]{3,0,2,1:T(8,128)S(1)}, f32[12,8,2,256]{3,0,2,1:T(8,128)S(1)}, u32[]{:S(2)}, u32[]{:S(2)}) collective-permute-start(f32[12,8,2,256]{3,0,2,1:T(8,128)S(1)} %get-tuple-element.117), channel_id=1, source_target_pairs={{4,0},{8,4},{12,8},{16,12},{20,16},{24,20},{28,24},{32,28},{36,32}... | collective-permute-start | bytes 589832 | tf_op jit(solution)/shard_map/ppermute | solution.py:21
  87.8 27.4 %collective-permute-start.3 = (f32[12,8,2,256]{3,0,2,1:T(8,128)S(1)}, f32[12,8,2,256]{3,0,2,1:T(8,128)S(1)}, u32[]{:S(2)}, u32[]{:S(2)}) collective-permute-start(f32[12,8,2,256]{3,0,2,1:T(8,128)S(1)} %get-tuple-element.116), channel_id=1, source_target_pairs={{0,4},{4,8},{8,12},{12,16},{16,20},{20,24},{24,28},{28,32},{32,36}... | collective-permute-start | bytes 589832 | tf_op jit(solution)/shard_map/ppermute | solution.py:19
  100.0 6.0 %collective-permute-start.10 = (f32[4,8,2,512]{3,0,2,1:T(4,128)S(1)}, f32[4,8,2,512]{3,0,2,1:T(4,128)S(1)}, u32[]{:S(2)}, u32[]{:S(2)}) collective-permute-start(f32[4,8,2,512]{3,0,2,1:T(4,128)S(1)} %get-tuple-element.79), channel_id=1, source_target_pairs={{4,0},{8,4},{12,8},{16,12},{20,16},{24,20},{28,24},{32,28},{36,32}... | collective-permute-start | bytes 393224 | tf_op jit(solution)/shard_map/ppermute | solution.py:21
  101.3 5.2 %collective-permute-start.11 = (f32[4,8,2,512]{3,0,2,1:T(4,128)S(1)}, f32[4,8,2,512]{3,0,2,1:T(4,128)S(1)}, u32[]{:S(2)}, u32[]{:S(2)}) collective-permute-start(f32[4,8,2,512]{3,0,2,1:T(4,128)S(1)} %get-tuple-element.78), channel_id=1, source_target_pairs={{0,4},{4,8},{8,12},{12,16},{16,20},{20,24},{24,28},{28,32},{32,36}... | collective-permute-start | bytes 393224 | tf_op jit(solution)/shard_map/ppermute | solution.py:19
  119.7 7.2 %collective-permute-start.4 = (f32[12,8,2,256]{3,0,2,1:T(8,128)S(1)}, f32[12,8,2,256]{3,0,2,1:T(8,128)S(1)}, u32[]{:S(2)}, u32[]{:S(2)}) collective-permute-start(f32[12,8,2,256]{3,0,2,1:T(8,128)S(1)} %get-tuple-element.109), channel_id=1, source_target_pairs={{4,0},{8,4},{12,8},{16,12},{20,16},{24,20},{28,24},{32,28},{36,32}... | collective-permute-start | bytes 589832 | tf_op jit(solution)/shard_map/ppermute | solution.py:21
  121.0 6.4 %collective-permute-start.5 = (f32[12,8,2,256]{3,0,2,1:T(8,128)S(1)}, f32[12,8,2,256]{3,0,2,1:T(8,128)S(1)}, u32[]{:S(2)}, u32[]{:S(2)}) collective-permute-start(f32[12,8,2,256]{3,0,2,1:T(8,128)S(1)} %get-tuple-element.108), channel_id=1, source_target_pairs={{0,4},{4,8},{8,12},{12,16},{16,20},{20,24},{24,28},{28,32},{32,36}... | collective-permute-start | bytes 589832 | tf_op jit(solution)/shard_map/ppermute | solution.py:19
  132.7 322.7 %all-gather.4.cloned.1.call-start = ((), (), s32[]{:S(2)}) async-start(), calls=%async_computation | async-start | bytes 2621440 | tf_op jit(solution)/shard_map/all_gather | solution.py:152
  192.9 2.5 copy-start.25
  195.4 280.4 %all-gather.6.cloned.1.call-start = ((), (), s32[]{:S(2)}) async-start(), calls=%async_computation.1 | async-start | bytes 5242880 | tf_op jit(solution)/shard_map/all_gather | solution.py:155
  205.9 5.4 %copy-start.18 = (f32[8,16,512]{2,1,0:T(8,128)S(1)}, f32[8,16,512]{2,1,0:T(8,128)}, u32[]{:S(2)}) copy-start(f32[8,16,512]{2,1,0:T(8,128)} %get-tuple-element.17) | copy-start | bytes 786436
  211.4 2.0 copy-start.13
  213.4 2.0 copy-start.28
  213.4 2.0 copy-start.29
  213.4 2.0 copy-start.30
  216.1 15.9 %copy-start.12 = (f32[4,8,8,256]{3,0,2,1:T(4,128)S(1)}, f32[4,8,8,256]{3,0,2,1:T(4,128)}, u32[]{:S(2)}) copy-start(f32[4,8,8,256]{3,0,2,1:T(4,128)} %copy-done.11) | copy-start | bytes 786436
  232.0 5.1 %copy-start.14 = (f32[8,16,512]{2,1,0:T(8,128)S(1)}, f32[8,16,512]{2,1,0:T(8,128)}, u32[]{:S(2)}) copy-start(f32[8,16,512]{2,1,0:T(8,128)} %copy-done.13) | copy-start | bytes 786436
  251.6 6.2 %copy-start.23 = (f32[8,2,8,128]{3,2,1,0:T(8,128)S(1)}, f32[8,2,8,128]{3,2,1,0:T(8,128)}, u32[]{:S(2)}) copy-start(f32[8,2,8,128]{3,2,1,0:T(8,128)} %get-tuple-element.128) | copy-start | bytes 196612
  264.1 6.2 %copy-start.24 = (f32[8,2,8,128]{3,2,1,0:T(8,128)S(1)}, f32[8,2,8,128]{3,2,1,0:T(8,128)}, u32[]{:S(2)}) copy-start(f32[8,2,8,128]{3,2,1,0:T(8,128)} %get-tuple-element.127) | copy-start | bytes 196612
  270.3 6.2 %copy-start.31 = (f32[1024]{0:T(1024)S(1)}, f32[1024]{0:T(1024)}, u32[]{:S(2)}) copy-start(f32[1024]{0:T(1024)} %param.18) | copy-start | bytes 12292
  270.3 6.2 %copy-start.32 = (f32[1024]{0:T(1024)S(1)}, f32[1024]{0:T(1024)}, u32[]{:S(2)}) copy-start(f32[1024]{0:T(1024)} %param.19) | copy-start | bytes 12292
  276.5 12.5 %copy-start.2 = (f32[8,8,8,256]{3,0,2,1:T(8,128)S(1)}, f32[8,8,8,256]{3,0,2,1:T(8,128)}, u32[]{:S(2)}) copy-start(f32[8,8,8,256]{3,0,2,1:T(8,128)} %subtract_multiply_fusion.1) | copy-start | bytes 1572868
  300.7 147.3 %copy-start.22 = (f32[8,8,256]{2,0,1:T(8,128)S(1)}, f32[8,8,256]{2,0,1:T(8,128)}, u32[]{:S(2)}) copy-start(f32[8,8,256]{2,0,1:T(8,128)} %copy.147) | copy-start | bytes 196612
  482.8 1.3 copy-start.1
  484.1 1.3 copy-start.17
  484.1 1.3 copy-start.19
  484.1 1.3 slice-start
  (1 other events, 0.7 us)
Sparse Core Ops, SparseCore 0:
  132.8 60.0 all-reduce.15
  195.5 31.3 all-gather.3
  229.2 48.2 all-gather.5
where the time goes:
time: 502 us; the launch traced here: 493 us
  local copies, waits for them, and re-layouts  161 us (32%)
  blocking collectives  148 us (29%)
  other arithmetic  62.5 us (12%)
  waiting for transfers between devices  61.3 us (12%)
  starting transfers between devices  33.6 us (7%)
  between operations  15.7 us (3%)
  matrix products  10.7 us (2%)
    psum x1, blocking collectives, per_device(): gram, rhs = lax.psum((gram_part, rhs_part), 'rows')  124 us
    psum x1, waiting for transfers between devices, per_device(): lax.psum((jnp.sum(fine, 0), jnp.sum(pair_c, 0), jnp.sum(level_c, 0)), 'mem')  60.2 us
    ppermute x6, starting transfers between devices, extended(): lax.ppermute(tail, axis, [(i, (i + 1) % count) for i in range(ends)])  25.7 us
    reshape x8, local copies, waits for them, and re-layouts, prolong(): return jnp.repeat(jnp.repeat(coarse, 2, axis=-2), 2, axis=-1)  23.1 us
    unnamed x78, local copies, waits for them, and re-layouts  19.4 us
    reduce_sum x1, other arithmetic, restrict(): return blocks.mean(axis=(-3, -1))  17.7 us
    broadcast_in_dim x8, local copies, waits for them, and re-layouts, prolong(): return jnp.repeat(jnp.repeat(coarse, 2, axis=-2), 2, axis=-1)  16.1 us
    reshape x1, local copies, waits for them, and re-layouts, per_device(): fine_anom.reshape(pairs_dev, -1)  15.9 us
  transfers between devices with their start and end apart: 15, of which 3 were waited for; matrix products, arithmetic and copies ran while one was open for 42% of the time, Pallas kernels for 0%

commit v1 on v0

v1 whole, which is shorter than its diff:
```python
import functools
import math

import jax
import jax.numpy as jnp
from jax import lax
from jax.experimental import pallas as pl
from jax.experimental.pallas import tpu as pltpu
from jax.sharding import PartitionSpec as P

STEPS = 3
HALO = 2 * STEPS
LANES = 128
MESH = pl.DeviceIdType.MESH
HIGHEST = lax.Precision.HIGHEST
F32 = jnp.float32
BF16 = jnp.bfloat16


def iota(shape, axis):
    return lax.broadcasted_iota(jnp.int32, shape, axis)


def halves(value):
    high = value.astype(BF16)
    return high, (value - high.astype(F32)).astype(BF16)


def dot(left, right):
    return jnp.dot(left, right, preferred_element_type=F32)


def exact_dot(left, right):
    return jnp.dot(left, right, precision=HIGHEST, preferred_element_type=F32)


def shifted(row):
    width = row.shape[-1]
    return pltpu.roll(row, 1, axis=1), pltpu.roll(row, width - 1, axis=1)


def layer_vector(ref, scale, layers, width):
    at = iota((layers, width), 0)
    out = jnp.zeros((layers, width), F32)
    for k in range(layers):
        out = jnp.where(at == k, ref[k] * scale, out)
    return out


def advance(reads, writes, count, first_row, grid_rows, coef):
    lap_c, hyp_c, drift_c, up_c, low_c = coef
    layers = up_c.shape[0]

    def inside(j):
        at = first_row + j
        return jnp.where((at >= 0) & (at < grid_rows), 1.0, 0.0).astype(F32)

    def start(read):
        q0, q1, q2, q3 = read(0), read(1), read(2), read(3)
        left, right = shifted(q1)
        f1 = (q2 + q0 + left + right - 4.0 * q1) * inside(1)
        left, right = shifted(q2)
        f2 = (q3 + q1 + left + right - 4.0 * q2) * inside(2)
        return f1, f2, right - left

    def one(i, carry, read, write):
        f1, f2, side = carry
        q2, q3, q4 = read(i + 2), read(i + 3), read(i + 4)
        left, right = shifted(q3)
        f3 = (q4 + q2 + left + right - 4.0 * q3) * inside(i + 3)
        fl, fr = shifted(f2)
        out = (
            0.8 * q2
            + up_c * pltpu.roll(q2, layers - 1, axis=0)
            + low_c * pltpu.roll(q2, 1, axis=0)
            + lap_c * f2
            - hyp_c * (f1 + f3 + fl + fr)
            - drift_c * side
        )
        write(i, out * inside(i + 2))
        return f2, f3, right - left

    unroll = 4

    def body(step, carries):
        carries = list(carries)
        for sub in range(unroll):
            for m in range(len(reads)):
                carries[m] = one(step * unroll + sub, carries[m], reads[m], writes[m])
        return tuple(carries)

    lax.fori_loop(0, count // unroll, body, tuple(start(read) for read in reads))


def cycle_kernel(
    sizes,
    fine_in,
    coarse_in,
    diff_ref,
    hyper_ref,
    drift_ref,
    val_ref,
    var_ref,
    row_ref,
    col_ref,
    layer_ref,
    count_ref,
    pair_out,
    mean_out,
    xv,
    zv,
    fq,
    cq,
    ft1,
    ft2,
    ct1,
    ct2,
    cres,
    g,
    ga,
    za,
    oc,
    rm,
    occ,
    rmc,
    sown,
    sx,
    ar0,
    ar1,
    kron_ref,
    inc,
    dg,
    dh,
    dl,
    mu,
    ob,
    mb,
    load_sem,
    hs_sem,
    hr_sem,
    ss_sem,
    sr_sem,
    as_sem,
    ar_sem,
    ts_sem,
    tr_sem,
    os_sem,
    or_sem,
    own_sem,
):
    tiles, groups, pairs, levels, K, RF, RC, NC, NCC, stages = sizes
    tile = lax.axis_index("rows")
    me = lax.axis_index("mem")
    level_all, pair_all = levels * groups, pairs * groups
    E = level_all + pair_all
    nv, nvc = NC // LANES, NCC // LANES
    lch, pch = levels // 2, pairs // 2
    RQ, RQC = RF // groups, RC // groups
    s_f, s_c = math.sqrt(pair_all - 1), math.sqrt(level_all - 1)

    def at(row, mem):
        return (row, mem)

    def mem_peer(i):
        return lax.rem(me + i, groups)

    def stage_peer(stage, i):
        stride, size = stage
        mine = lax.rem(tile // stride, size)
        return tile + (lax.rem(mine + i, size) - mine) * stride

    up = lax.rem(tile + tiles - 1, tiles)
    down = lax.rem(tile + 1, tiles)

    loads = []
    for v in range(nvc):
        loads.append(pltpu.make_async_copy(coarse_in.at[:, pl.ds(v * LANES, LANES)], zv.at[v], load_sem.at[v]))
    for v in range(nv):
        loads.append(pltpu.make_async_copy(fine_in.at[:, pl.ds(v * LANES, LANES)], xv.at[v], load_sem.at[nvc + v]))
    for load in loads:
        load.start()

    targets = [(up, me), (down, me)]
    targets += [(tile, mem_peer(i)) for i in range(1, groups)]
    for stage in stages:
        targets += [(stage_peer(stage, i), me) for i in range(1, stage[1])]
    barrier = pltpu.get_barrier_semaphore()
    for target in targets:
        pl.semaphore_signal(barrier, inc=1, device_id=at(*target), device_id_type=MESH)

    for load in loads[:nvc]:
        load.wait()

    def place_level(i, _):
        m, r = i // RC, lax.rem(i, RC)
        row = jnp.concatenate([zv[v, pl.ds(m * K * RC + r, K, stride=RC), :] for v in range(nvc)], 1)
        cq[m // 2, lax.rem(m, 2), HALO + r] = row
        return 0

    lax.fori_loop(0, levels * RC, place_level, 0)
    pl.semaphore_wait(barrier, len(targets))

    def coarse_halo(ch, way):
        src = HALO if way == 0 else RC
        dst = HALO + RC if way == 0 else 0
        return pltpu.make_async_remote_copy(
            src_ref=cq.at[ch, :, pl.ds(src, HALO)],
            dst_ref=cq.at[ch, :, pl.ds(dst, HALO)],
            send_sem=hs_sem.at[ch, way],
            recv_sem=hr_sem.at[ch, way],
            device_id=at(up if way == 0 else down, me),
            device_id_type=MESH,
        )

    def fine_halo(j, way):
        src = HALO if way == 0 else RF
        dst = HALO + RF if way == 0 else 0
        return pltpu.make_async_remote_copy(
            src_ref=fq.at[j, pl.ds(src, HALO)],
            dst_ref=fq.at[j, pl.ds(dst, HALO)],
            send_sem=hs_sem.at[lch + pch + j, way],
            recv_sem=hr_sem.at[lch + pch + j, way],
            device_id=at(up if way == 0 else down, me),
            device_id_type=MESH,
        )

    for ch in range(lch):
        for way in range(2):
            coarse_halo(ch, way).start()

    for load in loads[nvc:]:
        load.wait()

    halve = jnp.where(iota((NC, NCC), 0) // 2 == iota((NC, NCC), 1), 0.25, 0.0).astype(F32)
    widen = jnp.where(iota((NCC, NC), 1) // 2 == iota((NCC, NC), 0), 1.0, 0.0).astype(F32)
    widen_h = widen.astype(BF16)

    def place_fine(i, _):
        m, r = i // RF, lax.rem(i, RF)
        row = jnp.concatenate([xv[v, pl.ds(m * K * RF + r, K, stride=RF), :] for v in range(nv)], 1)
        fq[m, HALO + r] = row
        return 0

    lax.fori_loop(0, pairs * RF, place_fine, 0)
    for m in range(pairs):
        own = fq[m, HALO : HALO + RF].reshape(RC, 2, K, NC)
        rows = (own[:, 0] + own[:, 1]).reshape(RC * K, NC)
        cq[lch + m // 2, m % 2, HALO : HALO + RC] = exact_dot(rows, halve).reshape(RC, K, NCC)
    for ch in range(lch, lch + pch):
        for way in range(2):
            coarse_halo(ch, way).start()
    for j in range(pairs):
        for way in range(2):
            fine_halo(j, way).start()

    nb = 4
    per = val_ref.shape[0] * LANES // nb
    sub = per // LANES

    def row_of(ref, first, number):
        return jnp.concatenate([ref[i : i + 1, :] for i in range(first, first + number)], 1)

    for b in range(nb):
        col = row_of(col_ref, b * sub, sub)
        lay = row_of(layer_ref, b * sub, sub)
        loc = row_of(row_ref, b * sub, sub) - tile * RF
        oc[b] = jnp.where(iota((NC, per), 0) == col, 1.0, 0.0).astype(BF16)
        occ[b] = jnp.where(iota((NCC, per), 0) == (col >> 1), 1.0, 0.0).astype(BF16)
        rm[b] = jnp.where(iota((RF * K, per), 0) == loc * K + lay, 1.0, 0.0).astype(F32)
        rmc[b] = jnp.where(iota((RC * K, per), 0) == (loc >> 1) * K + lay, 1.0, 0.0).astype(F32)

    def coefs(scale_a, scale_h, scale_u, width):
        a = layer_vector(diff_ref, scale_a, K, width)
        h = layer_vector(hyper_ref, scale_h, K, width)
        u = layer_vector(drift_ref, scale_u, K, width)
        k = iota((K, width), 0)
        up_c = jnp.where(k < K - 1, 0.1, 0.0).astype(F32)
        low_c = jnp.where(k > 0, 0.1, 0.0).astype(F32)
        return a + 4.0 * h, h, 0.5 * u, up_c, low_c

    def zero_edges(clear_low, clear_high):
        @pl.when(tile == 0)
        def _():
            clear_low()

        @pl.when(tile == tiles - 1)
        def _():
            clear_high()

    coarse_coef = coefs(0.25, 0.0625, 0.5, NCC)
    row_c = tile * RC - HALO
    grid_c = tiles * RC

    def coarse_chunk(ch, _):
        coarse_halo(ch, 0).wait_recv()
        coarse_halo(ch, 1).wait_recv()

        def clear(first):
            cq[ch, :, first : first + HALO] = jnp.zeros((2, HALO, K, NCC), F32)

        zero_edges(lambda: clear(0), lambda: clear(HALO + RC))

        def reader(ref, m, lead):
            return lambda j: ref[lead + (m, j)]

        def writer(ref, m, lead):
            def write(i, value):
                ref[lead + (m, i)] = value
            return write

        both = range(2)
        advance([reader(cq, m, (ch,)) for m in both], [writer(ct1, m, ()) for m in both], RC + 8, row_c, grid_c, coarse_coef)
        advance([reader(ct1, m, ()) for m in both], [writer(ct2, m, ()) for m in both], RC + 4, row_c + 2, grid_c, coarse_coef)
        advance([reader(ct2, m, ()) for m in both], [writer(cres, m, (ch,)) for m in both], RC, row_c + 4, grid_c, coarse_coef)
        return 0

    lax.fori_loop(0, lch + pch, coarse_chunk, 0)

    def level_send(i):
        peer = mem_peer(i)
        return pltpu.make_async_remote_copy(
            src_ref=cres.at[pl.ds(0, lch), :, pl.ds(peer * RQC, RQC)],
            dst_ref=za.at[me],
            send_sem=ts_sem.at[0, i - 1],
            recv_sem=tr_sem.at[0, i - 1],
            device_id=at(tile, peer),
            device_id_type=MESH,
        )

    def pair_send(i):
        peer = mem_peer(i)
        return pltpu.make_async_remote_copy(
            src_ref=g.at[:, pl.ds(peer * RQ, RQ)],
            dst_ref=ga.at[me],
            send_sem=ts_sem.at[1, i - 1],
            recv_sem=tr_sem.at[1, i - 1],
            device_id=at(tile, peer),
            device_id_type=MESH,
        )

    for i in range(1, groups):
        level_send(i).start()

    fine_coef = coefs(1.0, 1.0, 1.0, NC)
    row_f = tile * RF - HALO
    grid_f = tiles * RF

    def fine_member(j, _):
        fine_halo(j, 0).wait_recv()
        fine_halo(j, 1).wait_recv()

        def clear(first):
            fq[j, first : first + HALO] = jnp.zeros((HALO, K, NC), F32)

        zero_edges(lambda: clear(0), lambda: clear(HALO + RF))

        def put(ref):
            def write(i, value):
                ref[i] = value
            return write

        def put_g(i, value):
            g[j, i] = value

        advance([lambda i: fq[j, i]], [put(ft1)], RF + 8, row_f, grid_f, fine_coef)
        advance([lambda i: ft1[i]], [put(ft2)], RF + 4, row_f + 2, grid_f, fine_coef)
        advance([lambda i: ft2[i]], [put_g], RF, row_f + 4, grid_f, fine_coef)
        coarse = cres[lch + j // 2, lax.rem(j, 2)].reshape(RC * K, NCC)
        wide = exact_dot(coarse, widen).reshape(RC, 1, K, NC)
        g[j] = (g[j].reshape(RC, 2, K, NC) - wide).reshape(RF, K, NC)
        return 0

    lax.fori_loop(0, pairs, fine_member, 0)

    def gather_block(b, _):
        high, low = halves(cres[0:lch].reshape(levels * RC * K, NCC))
        got = (dot(high, occ[b]) + dot(low, occ[b])).reshape(levels, RC * K, per)
        z = jnp.sum(got * rmc[b][None], axis=1)
        high, low = halves(g[...].reshape(pairs * RF * K, NC))
        got = (dot(high, oc[b]) + dot(low, oc[b])).reshape(pairs, RF * K, per)
        f = jnp.sum(got * rm[b][None], axis=1)
        rest = sown.shape[1] - levels - pairs
        sown[b] = jnp.concatenate([z, f, jnp.zeros((rest, per), F32)], 0)
        return 0

    lax.fori_loop(0, nb, gather_block, 0)

    def obs_send(i):
        return pltpu.make_async_remote_copy(
            src_ref=sown,
            dst_ref=sx.at[me],
            send_sem=ss_sem.at[i - 1],
            recv_sem=sr_sem.at[i - 1],
            device_id=at(tile, mem_peer(i)),
            device_id_type=MESH,
        )

    for i in range(1, groups):
        obs_send(i).start()
    for i in range(1, groups):
        pair_send(i).start()
    sx[me] = sown[...]
    own_level = pltpu.make_async_copy(cres.at[pl.ds(0, lch), :, pl.ds(me * RQC, RQC)], za.at[me], own_sem.at[0])
    own_pair = pltpu.make_async_copy(g.at[:, pl.ds(me * RQ, RQ)], ga.at[me], own_sem.at[1])
    own_level.start()
    own_pair.start()
    for i in range(1, groups):
        obs_send(i).wait_recv()

    gram = jnp.zeros((E + 8, E), F32)
    for b in range(nb):
        z = jnp.concatenate([sx[x, b, 0:levels] for x in range(groups)], 0)
        f = jnp.concatenate([sx[x, b, levels : levels + pairs] for x in range(groups)], 0)
        z_mean = jnp.mean(z, axis=0, keepdims=True)
        f_mean = jnp.mean(f, axis=0, keepdims=True)
        s = jnp.concatenate([(z - z_mean) * (1.0 / s_c), (f - f_mean) * (1.0 / s_f)], 0)
        innov = row_of(val_ref, b * sub, sub) - (z_mean + f_mean)
        slot = iota((1, per), 1) + b * per
        weight = jnp.where(slot < count_ref[0], 1.0 / row_of(var_ref, b * sub, sub), 0.0)
        extra = jnp.where(iota((8, per), 0) == 0, weight * innov, 0.0)
        left = jnp.concatenate([s * weight, extra], 0)
        gram = gram + lax.dot_general(
            left, s, (((1,), (1,)), ((), ())), precision=HIGHEST, preferred_element_type=F32
        )
    gram = jnp.concatenate([gram, jnp.zeros((E + 8, LANES - E), F32)], 1)

    slot0 = 0
    for s, stage in enumerate(stages):
        ar0[s] = gram
        sends = []
        for i in range(1, stage[1]):
            n = slot0 + i - 1
            send = pltpu.make_async_remote_copy(
                src_ref=ar0.at[s],
                dst_ref=ar1.at[n],
                send_sem=as_sem.at[n],
                recv_sem=ar_sem.at[n],
                device_id=at(stage_peer(stage, i), me),
                device_id_type=MESH,
            )
            send.start()
            sends.append((send, n))
        for send, n in sends:
            send.wait_recv()
            gram = gram + ar1[n]
        for send, n in sends:
            send.wait_send()
        slot0 += stage[1] - 1

    rows_t = E + pair_all + 8
    lane = iota((rows_t, LANES), 1)
    eye = jnp.where(iota((E, LANES), 0) == iota((E, LANES), 1), 1.0, 0.0).astype(F32)
    table = jnp.concatenate([gram[0:E] + eye, gram[level_all:E], gram[E:]], 0)
    for k in range(E):
        column = table[:, k : k + 1] * (1.0 / table[k : k + 1, k : k + 1])
        table = jnp.where(lane == k, column, table - column * table[k : k + 1, :])
    solved = jnp.concatenate([-0.5 * table[E : E + pair_all], table[E + pair_all :]], 0)

    spread = jnp.where(iota((LANES, E * K), 1) // K == iota((LANES, E * K), 0), 1.0, 0.0).astype(BF16)
    same = jnp.where(lax.rem(iota((K, E * K), 1), K) == iota((K, E * K), 0), 1.0, 0.0).astype(F32)
    coef_h, coef_l = halves(solved)

    def kron(part):
        wide = dot(part, spread)
        blocks = [wide[m : m + 1, :] * same for m in range(pair_all + 2)]
        return jnp.concatenate(blocks, 0).astype(BF16)

    kron_rows = kron_ref.shape[0] // 2
    kron_ref[0:kron_rows] = kron(coef_h)
    kron_ref[kron_rows:] = kron(coef_l)
    zk = level_all * K

    own_level.wait()
    own_pair.wait()
    for i in range(1, groups):
        level_send(i).wait_recv()
        pair_send(i).wait_recv()

    def anomalies(r, _):
        rc = r // 2
        z = za[:, :, :, rc].reshape(level_all, K, NCC)
        z_mean = jnp.mean(z, axis=0)
        high, low = halves(((z - z_mean[None]) * (1.0 / s_c)).reshape(zk, NCC))
        dh[r, 0:zk] = dot(high, widen_h).astype(BF16)
        dl[r, 0:zk] = dot(low, widen_h).astype(BF16)
        f = ga[:, :, r].reshape(pair_all, K, NC)
        f_mean = jnp.mean(f, axis=0)
        mu[r] = exact_dot(z_mean, widen) + f_mean
        anom = ((f - f_mean[None]) * (1.0 / s_f)).reshape(pair_all * K, NC)
        dg[r] = anom
        high, low = halves(anom)
        dh[r, zk:] = high
        dl[r, zk:] = low
        return 0

    lax.fori_loop(0, RQ, anomalies, 0)

    def result_send(r, i):
        peer = mem_peer(i)
        pair_copy = pltpu.make_async_remote_copy(
            src_ref=ob.at[pl.ds(peer * pairs, pairs), r],
            dst_ref=pair_out.at[:, me * RQ + r],
            send_sem=os_sem.at[0, r, i - 1],
            recv_sem=or_sem.at[0, r, i - 1],
            device_id=at(tile, peer),
            device_id_type=MESH,
        )
        mean_copy = pltpu.make_async_remote_copy(
            src_ref=mb.at[r],
            dst_ref=mean_out.at[me * RQ + r],
            send_sem=os_sem.at[1, r, i - 1],
            recv_sem=or_sem.at[1, r, i - 1],
            device_id=at(tile, peer),
            device_id_type=MESH,
        )
        return pair_copy, mean_copy

    np8 = pair_all * K

    def update(r, _):
        inc[...] = dot(kron_ref[...], dh[r])
        more = dot(kron_ref[0:kron_rows], dl[r])
        total = inc[0:kron_rows] + inc[kron_rows:] + more
        ob[:, r] = (s_f * (dg[r] + total[:np8])).reshape(pair_all, K, NC)
        mb[r] = mu[r] + total[np8 : np8 + K]
        for i in range(1, groups):
            for copy in result_send(r, i):
                copy.start()
        return 0

    lax.fori_loop(0, RQ, update, 0)
    own_out = pltpu.make_async_copy(ob.at[pl.ds(me * pairs, pairs)], pair_out.at[:, pl.ds(me * RQ, RQ)], own_sem.at[2])
    own_mean = pltpu.make_async_copy(mb, mean_out.at[pl.ds(me * RQ, RQ)], own_sem.at[3])
    own_out.start()
    own_mean.start()

    for ch in range(lch + pch):
        for way in range(2):
            coarse_halo(ch, way).wait_send()
    for j in range(pairs):
        for way in range(2):
            fine_halo(j, way).wait_send()
    for i in range(1, groups):
        level_send(i).wait_send()
        pair_send(i).wait_send()
        obs_send(i).wait_send()
    own_out.wait()
    own_mean.wait()
    for r in range(RQ):
        for i in range(1, groups):
            for copy in result_send(r, i):
                copy.wait_recv()
                copy.wait_send()


def order_kernel(K, RF, pair_in, mean_in, pair_out, mean_out, pv, mv, sem):
    nv = pv.shape[0]
    pairs = pair_in.shape[0]

    def put(value, ref, first, r):
        for v in range(nv):
            ref[v, pl.ds(first + r, K, stride=RF), :] = value[:, v * LANES : (v + 1) * LANES]

    def body(i, _):
        m, r = i // RF, lax.rem(i, RF)
        put(pair_in[m, r], pv, m * K * RF, r)
        return 0

    lax.fori_loop(0, pairs * RF, body, 0)

    def mean_body(r, _):
        put(mean_in[r], mv, 0, r)
        return 0

    lax.fori_loop(0, RF, mean_body, 0)
    copies = []
    for v in range(nv):
        copies.append(pltpu.make_async_copy(pv.at[v], pair_out.at[:, pl.ds(v * LANES, LANES)], sem.at[0, v]))
        copies.append(pltpu.make_async_copy(mv.at[v], mean_out.at[:, pl.ds(v * LANES, LANES)], sem.at[1, v]))
    for copy in copies:
        copy.start()
    for copy in copies:
        copy.wait()


def axis_stages(tiles):
    stages, stride = [], 1
    for size in (2, 4, 4):
        if stride < tiles:
            stages.append((stride, size))
            stride *= size
    return tuple(stages)


def per_device(
    fine_members,
    coarse_members,
    diffusion,
    hyper,
    drift,
    obs_value,
    obs_var,
    obs_row,
    obs_col,
    obs_layer,
    obs_count,
):
    tiles = lax.axis_size("rows")
    groups = lax.axis_size("mem")
    pairs, K, RF, NC = fine_members.shape
    levels, _, RC, NCC = coarse_members.shape
    stages = axis_stages(tiles)
    sizes = (tiles, groups, pairs, levels, K, RF, RC, NC, NCC, stages)
    slots = obs_value.shape[0]
    E = (pairs + levels) * groups
    nb = 4
    per = slots // nb
    RQ, RQC = RF // groups, RC // groups
    lch, pch = levels // 2, pairs // 2
    chunks = lch + pch + pairs
    peers = sum(size - 1 for _, size in stages)
    nv, nvc = NC // LANES, NCC // LANES
    srows = -(-(levels + pairs) // 8) * 8
    anyspace = pl.BlockSpec(memory_space=pl.ANY)
    vmem = pl.BlockSpec(memory_space=pltpu.VMEM)
    smem = pl.BlockSpec(memory_space=pltpu.SMEM)
    dma = pltpu.SemaphoreType.DMA

    def flat(obs):
        return obs.reshape(slots // LANES, LANES)

    pair_rows, mean_rows = pl.pallas_call(
        functools.partial(cycle_kernel, sizes),
        out_shape=(
            jax.ShapeDtypeStruct((pairs, RF, K, NC), F32),
            jax.ShapeDtypeStruct((RF, K, NC), F32),
        ),
        in_specs=[anyspace] * 2 + [smem] * 3 + [vmem] * 5 + [smem],
        out_specs=(anyspace, anyspace),
        scratch_shapes=[
            pltpu.VMEM((nv, pairs * K * RF, LANES), F32),
            pltpu.VMEM((nvc, levels * K * RC, LANES), F32),
            pltpu.VMEM((pairs, RF + 2 * HALO, K, NC), F32),
            pltpu.VMEM((lch + pch, 2, RC + 2 * HALO, K, NCC), F32),
            pltpu.VMEM((RF + 8, K, NC), F32),
            pltpu.VMEM((RF + 4, K, NC), F32),
            pltpu.VMEM((2, RC + 8, K, NCC), F32),
            pltpu.VMEM((2, RC + 4, K, NCC), F32),
            pltpu.VMEM((lch + pch, 2, RC, K, NCC), F32),
            pltpu.VMEM((pairs, RF, K, NC), F32),
            pltpu.VMEM((groups, pairs, RQ, K, NC), F32),
            pltpu.VMEM((groups, lch, 2, RQC, K, NCC), F32),
            pltpu.VMEM((nb, NC, per), BF16),
            pltpu.VMEM((nb, RF * K, per), F32),
            pltpu.VMEM((nb, NCC, per), BF16),
            pltpu.VMEM((nb, RC * K, per), F32),
            pltpu.VMEM((nb, srows, per), F32),
            pltpu.VMEM((groups, nb, srows, per), F32),
            pltpu.VMEM((len(stages), E + 8, LANES), F32),
            pltpu.VMEM((peers, E + 8, LANES), F32),
            pltpu.VMEM((2 * (pairs * groups + 2) * K, E * K), BF16),
            pltpu.VMEM((2 * (pairs * groups + 2) * K, NC), F32),
            pltpu.VMEM((RQ, pairs * groups * K, NC), F32),
            pltpu.VMEM((RQ, E * K, NC), BF16),
            pltpu.VMEM((RQ, E * K, NC), BF16),
            pltpu.VMEM((RQ, K, NC), F32),
            pltpu.VMEM((pairs * groups, RQ, K, NC), F32),
            pltpu.VMEM((RQ, K, NC), F32),
            dma((nv + nvc,)),
            dma((chunks, 2)),
            dma((chunks, 2)),
            dma((groups - 1,)),
            dma((groups - 1,)),
            dma((peers,)),
            dma((peers,)),
            dma((2, groups - 1)),
            dma((2, groups - 1)),
            dma((2, RQ, groups - 1)),
            dma((2, RQ, groups - 1)),
            dma((4,)),
        ],
        compiler_params=pltpu.CompilerParams(
            collective_id=0, has_side_effects=True, vmem_limit_bytes=48 * 1024 * 1024
        ),
        name="cycle",
    )(
        fine_members.reshape(pairs * K * RF, NC),
        coarse_members.reshape(levels * K * RC, NCC),
        diffusion,
        hyper,
        drift,
        flat(obs_value),
        flat(obs_var),
        flat(obs_row),
        flat(obs_col),
        flat(obs_layer),
        obs_count,
    )
    pair, mean = pl.pallas_call(
        functools.partial(order_kernel, K, RF),
        out_shape=(
            jax.ShapeDtypeStruct((pairs * K * RF, NC), F32),
            jax.ShapeDtypeStruct((K * RF, NC), F32),
        ),
        in_specs=[vmem, vmem],
        out_specs=(anyspace, anyspace),
        scratch_shapes=[
            pltpu.VMEM((nv, pairs * K * RF, LANES), F32),
            pltpu.VMEM((nv, K * RF, LANES), F32),
            dma((2, nv)),
        ],
        compiler_params=pltpu.CompilerParams(vmem_limit_bytes=16 * 1024 * 1024),
        name="order",
    )(pair_rows, mean_rows)
    return mean.reshape(K, RF, NC), pair.reshape(pairs, K, RF, NC)


def solution(mesh):
    in_specs = (
        P("mem", None, "rows", None),
        P("mem", None, "rows", None),
        P(),
        P(),
        P(),
        P("rows"),
        P("rows"),
        P("rows"),
        P("rows"),
        P("rows"),
        P("rows"),
    )
    out_specs = (P(None, "rows", None), P("mem", None, "rows", None))
    return jax.shard_map(
        per_device, mesh=mesh, in_specs=in_specs, out_specs=out_specs, check_vma=False
    )
```

time: 502 us -> 88.4 us (0.18); the launches traced: 493 us -> 87.6 us
  local copies, waits for them, and re-layouts: 161 us -> 4.32 us
  blocking collectives: 148 us -> 0 us
  Pallas kernels: 0 us -> 81.9 us
  other arithmetic: 62.5 us -> 0 us
  waiting for transfers between devices: 61.3 us -> 0 us
  starting transfers between devices: 33.6 us -> 0 us
  between operations: 15.7 us -> 1.36 us
  matrix products: 10.7 us -> 0 us
    psum x1 -> x0, blocking collectives: 124 us -> none  [per_device(): gram, rhs = lax.psum((gram_part, rhs_part), 'rows')]
    pallas_call x0 -> x2, Pallas kernels: none -> 81.9 us  [the longest x1 79.9 us: per_device(): pl.pallas_call(functools.partial(cycle_kernel, sizes), out_shape=(jax.Sha...]
    psum x1 -> x0, waiting for transfers between devices: 60.2 us -> none  [per_device(): lax.psum((jnp.sum(fine, 0), jnp.sum(pair_c, 0), jnp.sum(level_c, 0)), 'mem')]
    reshape x11 -> x0, local copies, waits for them, and re-layouts: 49.3 us -> none  [the longest x8 23.1 us: prolong(): return jnp.repeat(jnp.repeat(coarse, 2, axis=-2), 2, axis=-1)]
    gather x6 -> x0, local copies, waits for them, and re-layouts: 45.3 us -> none  [the longest x1 14.4 us: per_device(): jnp.take(fine_anom.reshape(pairs_dev, -1), fine_index, axis=1)]
    ppermute x12 -> x0, starting transfers between devices: 33.4 us -> none  [the longest x6 25.7 us: extended(): lax.ppermute(tail, axis, [(i, (i + 1) % count) for i in range(ends)])]
    slice x55 -> x0, local copies, waits for them, and re-layouts: 24.4 us -> none  [the longest x12 8.56 us: advance(): side = jnp.roll(centre, -1, axis=3) - jnp.roll(centre, 1, axis=3)]
    all_gather x2 -> x0, blocking collectives: 23.9 us -> none  [the longest x1 12 us: per_device(): lax.all_gather(level_obs, 'mem', axis=0, tiled=True)]
  transfers between devices with their start and end apart: 15 -> 0, of which waited for: 3 -> 0; matrix products, arithmetic and copies ran while one was open for 42% -> 0% of each run, Pallas kernels for 0% -> 0%
where the time goes in v1:
time: 88.4 us; the launch traced here: 87.6 us
  Pallas kernels  81.9 us (93%)
  local copies, waits for them, and re-layouts  4.32 us (5%)
  between operations  1.36 us (2%)
    pallas_call x1, Pallas kernels, per_device(): pl.pallas_call(functools.partial(cycle_kernel, sizes), out_shape=(jax.Sha...  79.9 us
    unnamed x20, local copies, waits for them, and re-layouts  4.32 us
    pallas_call x1, Pallas kernels, per_device(): pl.pallas_call(functools.partial(order_kernel, K, RF), out_shape=(jax.Sha...  2.09 us

profile of v1, /device:TPU:0, one launch (start us, length us, event | category | flops | bytes accessed | tf_op | source)
XLA Modules:
  0.0 87.6 jit_solution(13719621286692118182)
XLA Ops:
  0.6 0.0 copy-start.9
  1.3 0.0 copy-start.4
  1.3 0.0 copy-start.3
  1.3 0.0 copy-start.2
  1.3 0.0 copy-start.7
  1.3 0.0 copy-start.8
  1.4 0.0 copy-done.9
  1.4 0.6 copy-done.4
  2.0 0.0 copy-done.3
  2.0 0.0 copy-done.2
  2.0 0.0 copy-done.7
  2.0 0.0 copy-done.8
  2.0 0.0 copy-start
  2.0 1.2 %copy-done = f32[4,8,16,512]{3,2,1,0:T(8,128)S(1)} copy-done((f32[4,8,16,512]{3,2,1,0:T(8,128)S(1)}, f32[4,8,16,512]{3,2,1,0:T(8,128)}, u32[]{:S(2)}) %copy-start) | copy-done | bytes 1048600
  3.3 0.0 copy-start.1
  3.3 1.0 %copy-done.1 = f32[8,8,8,256]{3,2,1,0:T(8,128)S(1)} copy-done((f32[8,8,8,256]{3,2,1,0:T(8,128)S(1)}, f32[8,8,8,256]{3,2,1,0:T(8,128)}, u32[]{:S(2)}) %copy-start.1) | copy-done | bytes 524312
  4.3 0.0 copy-start.5
  4.3 0.7 copy-done.5
  5.0 0.0 copy-start.6
  5.0 0.7 copy-done.6
  5.7 79.9 %cycle.1 = (f32[4,16,8,512]{3,2,1,0:T(8,128)S(1)}, f32[16,8,512]{2,1,0:T(8,128)S(1)}) custom-call(f32[512,512]{1,0:T(8,128)S(1)} %bitcast.9, f32[512,256]{1,0:T(8,128)S(1)} %bitcast.10, f32[8]{0:T(128)S(1)} %copy-done.7, f32[8]{0:T(128)S(1)} %copy-done.8, f32[8]{0:T(128)S(1)} %copy-done.9, f32[8,128]{1,0:T(8,128)S(1)} %bitcast.11, f32[8,128]{1,0:T(8,128)S(1)} %bitcast.12, ...), custom_call_target="tpu_custom_call" | custom-call | tf_op jit(solution)/shard_map/cycle/pallas_call | solution.py:632
  85.5 2.1 %order.1 = (f32[512,512]{1,0:T(8,128)}, f32[128,512]{1,0:T(8,128)}) custom-call(f32[4,16,8,512]{3,2,1,0:T(8,128)S(1)} %get-tuple-element.6.pair_in, f32[16,8,512]{2,1,0:T(8,128)S(1)} %get-tuple-element.7.mean_in), custom_call_target="tpu_custom_call" | custom-call | tf_op jit(solution)/shard_map/order/pallas_call | solution.py:699
Async XLA Ops:
  0.6 0.7 copy-start.9
  1.3 0.7 copy-start.4
  1.3 0.7 copy-start.3
  1.3 0.7 copy-start.2
  1.3 0.7 copy-start.7
  1.3 0.7 copy-start.8
  2.0 1.2 %copy-start = (f32[4,8,16,512]{3,2,1,0:T(8,128)S(1)}, f32[4,8,16,512]{3,2,1,0:T(8,128)}, u32[]{:S(2)}) copy-start(f32[4,8,16,512]{3,2,1,0:T(8,128)} %param.11) | copy-start | bytes 3145732
  3.3 1.0 %copy-start.1 = (f32[8,8,8,256]{3,2,1,0:T(8,128)S(1)}, f32[8,8,8,256]{3,2,1,0:T(8,128)}, u32[]{:S(2)}) copy-start(f32[8,8,8,256]{3,2,1,0:T(8,128)} %param.12) | copy-start | bytes 1572868
  4.3 0.7 copy-start.5
  5.0 0.7 copy-start.6

commit v2 on v1

--- a/solution.py
+++ b/solution.py
@@ -30,8 +30,14 @@
     return jnp.dot(left, right, preferred_element_type=F32)
 
 
-def exact_dot(left, right):
-    return jnp.dot(left, right, precision=HIGHEST, preferred_element_type=F32)
+def select_dot(left, right):
+    rows = left.shape[0]
+    high = left.astype(BF16)
+    rest = left - high.astype(F32)
+    mid = rest.astype(BF16)
+    low = (rest - mid.astype(F32)).astype(BF16)
+    out = dot(jnp.concatenate([high, mid, low], 0), right)
+    return out[:rows] + (out[rows : 2 * rows] + out[2 * rows :])
 
 
 def shifted(row):
@@ -80,33 +86,36 @@
         write(i, out * inside(i + 2))
         return f2, f3, right - left
 
-    unroll = 4
-
-    def body(step, carries):
-        carries = list(carries)
-        for sub in range(unroll):
-            for m in range(len(reads)):
-                carries[m] = one(step * unroll + sub, carries[m], reads[m], writes[m])
-        return tuple(carries)
-
-    lax.fori_loop(0, count // unroll, body, tuple(start(read) for read in reads))
+    carries = [start(read) for read in reads]
+    for i in range(count):
+        for m in range(len(reads)):
+            carries[m] = one(i, carries[m], reads[m], writes[m])
 
 
 def cycle_kernel(
     sizes,
     fine_in,
     coarse_in,
+    diff_in,
+    hyper_in,
+    drift_in,
+    val_in,
+    var_in,
+    row_in,
+    col_in,
+    layer_in,
+    count_in,
+    pair_out,
+    mean_out,
     diff_ref,
     hyper_ref,
     drift_ref,
+    count_ref,
     val_ref,
     var_ref,
     row_ref,
     col_ref,
     layer_ref,
-    count_ref,
-    pair_out,
-    mean_out,
     xv,
     zv,
     fq,
@@ -136,6 +145,7 @@
     ob,
     mb,
     load_sem,
+    small_sem,
     hs_sem,
     hr_sem,
     ss_sem,
@@ -179,6 +189,20 @@
         loads.append(pltpu.make_async_copy(fine_in.at[:, pl.ds(v * LANES, LANES)], xv.at[v], load_sem.at[nvc + v]))
     for load in loads:
         load.start()
+    smalls = [
+        (diff_in, diff_ref),
+        (hyper_in, hyper_ref),
+        (drift_in, drift_ref),
+        (count_in, count_ref),
+        (val_in, val_ref),
+        (var_in, var_ref),
+        (row_in, row_ref),
+        (col_in, col_ref),
+        (layer_in, layer_ref),
+    ]
+    smalls = [pltpu.make_async_copy(a, b, small_sem.at[n]) for n, (a, b) in enumerate(smalls)]
+    for small in smalls:
+        small.start()
 
     targets = [(up, me), (down, me)]
     targets += [(tile, mem_peer(i)) for i in range(1, groups)]
@@ -191,13 +215,13 @@
     for load in loads[:nvc]:
         load.wait()
 
-    def place_level(i, _):
-        m, r = i // RC, lax.rem(i, RC)
-        row = jnp.concatenate([zv[v, pl.ds(m * K * RC + r, K, stride=RC), :] for v in range(nvc)], 1)
-        cq[m // 2, lax.rem(m, 2), HALO + r] = row
+    def place_level(m, _):
+        for r in range(RC):
+            row = jnp.concatenate([zv[v, pl.ds(m * K * RC + r, K, stride=RC), :] for v in range(nvc)], 1)
+            cq[m // 2, lax.rem(m, 2), HALO + r] = row
         return 0
 
-    lax.fori_loop(0, levels * RC, place_level, 0)
+    lax.fori_loop(0, levels, place_level, 0)
     pl.semaphore_wait(barrier, len(targets))
 
     def coarse_halo(ch, way):
@@ -231,21 +255,19 @@
     for load in loads[nvc:]:
         load.wait()
 
-    halve = jnp.where(iota((NC, NCC), 0) // 2 == iota((NC, NCC), 1), 0.25, 0.0).astype(F32)
-    widen = jnp.where(iota((NCC, NC), 1) // 2 == iota((NCC, NC), 0), 1.0, 0.0).astype(F32)
-    widen_h = widen.astype(BF16)
-
-    def place_fine(i, _):
-        m, r = i // RF, lax.rem(i, RF)
-        row = jnp.concatenate([xv[v, pl.ds(m * K * RF + r, K, stride=RF), :] for v in range(nv)], 1)
-        fq[m, HALO + r] = row
-        return 0
-
-    lax.fori_loop(0, pairs * RF, place_fine, 0)
-    for m in range(pairs):
+    halve = jnp.where(iota((NC, NCC), 0) // 2 == iota((NC, NCC), 1), 0.25, 0.0).astype(BF16)
+    widen = jnp.where(iota((NCC, NC), 1) // 2 == iota((NCC, NC), 0), 1.0, 0.0).astype(BF16)
+
+    def place_fine(m, _):
+        for r in range(RF):
+            row = jnp.concatenate([xv[v, pl.ds(m * K * RF + r, K, stride=RF), :] for v in range(nv)], 1)
+            fq[m, HALO + r] = row
         own = fq[m, HALO : HALO + RF].reshape(RC, 2, K, NC)
         rows = (own[:, 0] + own[:, 1]).reshape(RC * K, NC)
-        cq[lch + m // 2, m % 2, HALO : HALO + RC] = exact_dot(rows, halve).reshape(RC, K, NCC)
+        cq[lch + m // 2, lax.rem(m, 2), HALO : HALO + RC] = select_dot(rows, halve).reshape(RC, K, NCC)
+        return 0
+
+    lax.fori_loop(0, pairs, place_fine, 0)
     for ch in range(lch, lch + pch):
         for way in range(2):
             coarse_halo(ch, way).start()
@@ -253,6 +275,8 @@
         for way in range(2):
             fine_halo(j, way).start()
 
+    for small in smalls:
+        small.wait()
     nb = 4
     per = val_ref.shape[0] * LANES // nb
     sub = per // LANES
@@ -366,7 +390,7 @@
         advance([lambda i: ft1[i]], [put(ft2)], RF + 4, row_f + 2, grid_f, fine_coef)
         advance([lambda i: ft2[i]], [put_g], RF, row_f + 4, grid_f, fine_coef)
         coarse = cres[lch + j // 2, lax.rem(j, 2)].reshape(RC * K, NCC)
-        wide = exact_dot(coarse, widen).reshape(RC, 1, K, NC)
+        wide = select_dot(coarse, widen).reshape(RC, 1, K, NC)
         g[j] = (g[j].reshape(RC, 2, K, NC) - wide).reshape(RF, K, NC)
         return 0
 
@@ -424,6 +448,27 @@
         )
     gram = jnp.concatenate([gram, jnp.zeros((E + 8, LANES - E), F32)], 1)
 
+    zk = level_all * K
+
+    def level_anomalies():
+        own_level.wait()
+        for i in range(1, groups):
+            level_send(i).wait_recv()
+
+        def one(rc, _):
+            z = za[:, :, :, rc].reshape(level_all, K, NCC)
+            z_mean = jnp.mean(z, axis=0)
+            high, low = halves(((z - z_mean[None]) * (1.0 / s_c)).reshape(zk, NCC))
+            high, low = dot(high, widen).astype(BF16), dot(low, widen).astype(BF16)
+            wide_mean = select_dot(z_mean, widen)
+            for half in range(2):
+                dh[2 * rc + half, 0:zk] = high
+                dl[2 * rc + half, 0:zk] = low
+                mu[2 * rc + half] = wide_mean
+            return 0
+
+        lax.fori_loop(0, RQC, one, 0)
+
     slot0 = 0
     for s, stage in enumerate(stages):
         ar0[s] = gram
@@ -440,6 +485,8 @@
             )
             send.start()
             sends.append((send, n))
+        if s == 0:
+            level_anomalies()
         for send, n in sends:
             send.wait_recv()
             gram = gram + ar1[n]
@@ -451,9 +498,35 @@
     lane = iota((rows_t, LANES), 1)
     eye = jnp.where(iota((E, LANES), 0) == iota((E, LANES), 1), 1.0, 0.0).astype(F32)
     table = jnp.concatenate([gram[0:E] + eye, gram[level_all:E], gram[E:]], 0)
-    for k in range(E):
-        column = table[:, k : k + 1] * (1.0 / table[k : k + 1, k : k + 1])
-        table = jnp.where(lane == k, column, table - column * table[k : k + 1, :])
+    width = 4
+    for k in range(0, E, width):
+        block = range(width)
+        columns = [jnp.broadcast_to(table[:, k + i : k + i + 1], (rows_t, LANES)) for i in block]
+        heads = [table[k + i : k + i + 1, :] for i in block]
+        inv = [[columns[j][k + i : k + i + 1, :] for j in block] for i in block]
+        for p in block:
+            pivot = 1.0 / inv[p][p]
+            scaled = [pivot if j == p else inv[p][j] * pivot for j in block]
+            inv = [
+                scaled
+                if i == p
+                else [
+                    -inv[i][p] * pivot if j == p else inv[i][j] - inv[i][p] * scaled[j] for j in block
+                ]
+                for i in block
+            ]
+        ends = []
+        for i in block:
+            end = columns[0] * inv[0][i]
+            for j in range(1, width):
+                end = end + columns[j] * inv[j][i]
+            ends.append(end)
+        change = ends[0] * heads[0]
+        for i in range(1, width):
+            change = change + ends[i] * heads[i]
+        table = table - change
+        for i in block:
+            table = jnp.where(lane == k + i, ends[i], table)
     solved = jnp.concatenate([-0.5 * table[E : E + pair_all], table[E + pair_all :]], 0)
 
     spread = jnp.where(iota((LANES, E * K), 1) // K == iota((LANES, E * K), 0), 1.0, 0.0).astype(BF16)
@@ -468,24 +541,15 @@
     kron_rows = kron_ref.shape[0] // 2
     kron_ref[0:kron_rows] = kron(coef_h)
     kron_ref[kron_rows:] = kron(coef_l)
-    zk = level_all * K
-
-    own_level.wait()
+
     own_pair.wait()
     for i in range(1, groups):
-        level_send(i).wait_recv()
         pair_send(i).wait_recv()
 
-    def anomalies(r, _):
-        rc = r // 2
-        z = za[:, :, :, rc].reshape(level_all, K, NCC)
-        z_mean = jnp.mean(z, axis=0)
-        high, low = halves(((z - z_mean[None]) * (1.0 / s_c)).reshape(zk, NCC))
-        dh[r, 0:zk] = dot(high, widen_h).astype(BF16)
-        dl[r, 0:zk] = dot(low, widen_h).astype(BF16)
+    def pair_anomalies(r, _):
         f = ga[:, :, r].reshape(pair_all, K, NC)
         f_mean = jnp.mean(f, axis=0)
-        mu[r] = exact_dot(z_mean, widen) + f_mean
+        mu[r] = mu[r] + f_mean
         anom = ((f - f_mean[None]) * (1.0 / s_f)).reshape(pair_all * K, NC)
         dg[r] = anom
         high, low = halves(anom)
@@ -493,7 +557,7 @@
         dl[r, zk:] = low
         return 0
 
-    lax.fori_loop(0, RQ, anomalies, 0)
+    lax.fori_loop(0, RQ, pair_anomalies, 0)
 
     def result_send(r, i):
         peer = mem_peer(i)
@@ -561,24 +625,25 @@
         for v in range(nv):
             ref[v, pl.ds(first + r, K, stride=RF), :] = value[:, v * LANES : (v + 1) * LANES]
 
-    def body(i, _):
-        m, r = i // RF, lax.rem(i, RF)
-        put(pair_in[m, r], pv, m * K * RF, r)
-        return 0
-
-    lax.fori_loop(0, pairs * RF, body, 0)
-
-    def mean_body(r, _):
+    copies = []
+
+    def send(ref, first, out, row):
+        for v in range(nv):
+            copy = pltpu.make_async_copy(
+                ref.at[v, pl.ds(first, K * RF)],
+                out.at[pl.ds(first, K * RF), pl.ds(v * LANES, LANES)],
+                sem.at[row, v],
+            )
+            copy.start()
+            copies.append(copy)
+
+    for m in range(pairs):
+        for r in range(RF):
+            put(pair_in[m, r], pv, m * K * RF, r)
+        send(pv, m * K * RF, pair_out, m)
+    for r in range(RF):
         put(mean_in[r], mv, 0, r)
-        return 0
-
-    lax.fori_loop(0, RF, mean_body, 0)
-    copies = []
-    for v in range(nv):
-        copies.append(pltpu.make_async_copy(pv.at[v], pair_out.at[:, pl.ds(v * LANES, LANES)], sem.at[0, v]))
-        copies.append(pltpu.make_async_copy(mv.at[v], mean_out.at[:, pl.ds(v * LANES, LANES)], sem.at[1, v]))
-    for copy in copies:
-        copy.start()
+    send(mv, 0, mean_out, pairs)
     for copy in copies:
         copy.wait()
 
@@ -622,12 +687,15 @@
     nv, nvc = NC // LANES, NCC // LANES
     srows = -(-(levels + pairs) // 8) * 8
     anyspace = pl.BlockSpec(memory_space=pl.ANY)
+    hbm = pl.BlockSpec(memory_space=pltpu.HBM)
     vmem = pl.BlockSpec(memory_space=pltpu.VMEM)
-    smem = pl.BlockSpec(memory_space=pltpu.SMEM)
     dma = pltpu.SemaphoreType.DMA
 
     def flat(obs):
         return obs.reshape(slots // LANES, LANES)
+
+    def keep(array):
+        return pltpu.with_memory_space_constraint(array, pltpu.HBM)
 
     pair_rows, mean_rows = pl.pallas_call(
         functools.partial(cycle_kernel, sizes),
@@ -635,9 +703,18 @@
             jax.ShapeDtypeStruct((pairs, RF, K, NC), F32),
             jax.ShapeDtypeStruct((RF, K, NC), F32),
         ),
-        in_specs=[anyspace] * 2 + [smem] * 3 + [vmem] * 5 + [smem],
+        in_specs=[hbm] * 11,
         out_specs=(anyspace, anyspace),
         scratch_shapes=[
+            pltpu.SMEM((K,), F32),
+            pltpu.SMEM((K,), F32),
+            pltpu.SMEM((K,), F32),
+            pltpu.SMEM((1,), jnp.int32),
+            pltpu.VMEM((slots // LANES, LANES), F32),
+            pltpu.VMEM((slots // LANES, LANES), F32),
+            pltpu.VMEM((slots // LANES, LANES), jnp.int32),
+            pltpu.VMEM((slots // LANES, LANES), jnp.int32),
+            pltpu.VMEM((slots // LANES, LANES), jnp.int32),
             pltpu.VMEM((nv, pairs * K * RF, LANES), F32),
             pltpu.VMEM((nvc, levels * K * RC, LANES), F32),
             pltpu.VMEM((pairs, RF + 2 * HALO, K, NC), F32),
@@ -667,6 +744,7 @@
             pltpu.VMEM((pairs * groups, RQ, K, NC), F32),
             pltpu.VMEM((RQ, K, NC), F32),
             dma((nv + nvc,)),
+            dma((9,)),
             dma((chunks, 2)),
             dma((chunks, 2)),
             dma((groups - 1,)),
@@ -684,16 +762,16 @@
         ),
         name="cycle",
     )(
-        fine_members.reshape(pairs * K * RF, NC),
-        coarse_members.reshape(levels * K * RC, NCC),
-        diffusion,
-        hyper,
-        drift,
-        flat(obs_value),
-        flat(obs_var),
-        flat(obs_row),
-        flat(obs_col),
-        flat(obs_layer),
+        keep(fine_members.reshape(pairs * K * RF, NC)),
+        keep(coarse_members.reshape(levels * K * RC, NCC)),
+        keep(diffusion),
+        keep(hyper),
+        keep(drift),
+        keep(flat(obs_value)),
+        keep(flat(obs_var)),
+        keep(flat(obs_row)),
+        keep(flat(obs_col)),
+        keep(flat(obs_layer)),
         obs_count,
     )
     pair, mean = pl.pallas_call(
@@ -707,7 +785,7 @@
         scratch_shapes=[
             pltpu.VMEM((nv, pairs * K * RF, LANES), F32),
             pltpu.VMEM((nv, K * RF, LANES), F32),
-            dma((2, nv)),
+            dma((pairs + 1, nv)),
         ],
         compiler_params=pltpu.CompilerParams(vmem_limit_bytes=16 * 1024 * 1024),
         name="order",

time: 88.4 us -> 74.6 us (0.84)
  Pallas kernels: 81.9 us -> 72.7 us
  local copies, waits for them, and re-layouts: 4.32 us -> 0 us
    pallas_call x1, Pallas kernels: 79.9 us -> 71.3 us  [per_device(): pl.pallas_call(functools.partial(cycle_kernel, sizes), out_shape=(jax.Sha...]
    unnamed x20 -> x0, local copies, waits for them, and re-layouts: 4.32 us -> none
where the time goes in v2:
time: 74.6 us; the launch traced here: 74 us
  Pallas kernels  72.7 us (97%)
  between operations  1.29 us (2%)
    pallas_call x1, Pallas kernels, per_device(): pl.pallas_call(functools.partial(cycle_kernel, sizes), out_shape=(jax.Sha...  71.3 us

profile of v2, /device:TPU:0, one launch (start us, length us, event | category | flops | bytes accessed | tf_op | source)
XLA Modules:
  0.0 74.0 jit_solution(8067145157402796858)
XLA Ops:
  1.3 71.3 %cycle.1 = (f32[4,16,8,512]{3,2,1,0:T(8,128)S(1)}, f32[16,8,512]{2,1,0:T(8,128)S(1)}) custom-call(f32[512,512]{1,0:T(8,128)} %bitcast.9, f32[512,256]{1,0:T(8,128)} %bitcast.10, f32[8]{0:T(128)} %diff_in.1, f32[8]{0:T(128)} %hyper_in.1, f32[8]{0:T(128)} %drift_in.1, f32[8,128]{1,0:T(8,128)} %bitcast.11, f32[8,128]{1,0:T(8,128)} %bitcast.12, ...), custom_call_target="tpu_custom_call" | custom-call | tf_op jit(solution)/shard_map/cycle/pallas_call | solution.py:700
  72.6 1.4 %order.1 = (f32[512,512]{1,0:T(8,128)}, f32[128,512]{1,0:T(8,128)}) custom-call(f32[4,16,8,512]{3,2,1,0:T(8,128)S(1)} %get-tuple-element.6.pair_in, f32[16,8,512]{2,1,0:T(8,128)S(1)} %get-tuple-element.7.mean_in), custom_call_target="tpu_custom_call" | custom-call | tf_op jit(solution)/shard_map/order/pallas_call | solution.py:777

commit v3 on v2

--- a/solution.py
+++ b/solution.py
@@ -40,9 +40,31 @@
     return out[:rows] + (out[rows : 2 * rows] + out[2 * rows :])
 
 
+def column_at(place, parts):
+    return (place % LANES) * parts + place // LANES
+
+
+def place_of(column, parts):
+    shift = parts.bit_length() - 1
+    return (column & (parts - 1)) * LANES + (column >> shift)
+
+
 def shifted(row):
     width = row.shape[-1]
-    return pltpu.roll(row, 1, axis=1), pltpu.roll(row, width - 1, axis=1)
+    first, last = row[:, :LANES], row[:, width - LANES :]
+    left = jnp.concatenate([pltpu.roll(last, 1, axis=1), row[:, : width - LANES]], 1)
+    right = jnp.concatenate([row[:, LANES:], pltpu.roll(first, LANES - 1, axis=1)], 1)
+    return left, right
+
+
+def halved(row):
+    tiles = [row[:, i * LANES : (i + 1) * LANES] for i in range(row.shape[1] // LANES)]
+    return jnp.concatenate([a + b for a, b in zip(tiles[::2], tiles[1::2])], 1)
+
+
+def doubled(row):
+    tiles = [row[:, i * LANES : (i + 1) * LANES] for i in range(row.shape[1] // LANES)]
+    return jnp.concatenate([tile for tile in tiles for _ in range(2)], 1)
 
 
 def layer_vector(ref, scale, layers, width):
@@ -126,6 +148,7 @@
     ct2,
     cres,
     g,
+    gn,
     ga,
     za,
     oc,
@@ -164,7 +187,7 @@
     level_all, pair_all = levels * groups, pairs * groups
     E = level_all + pair_all
     nv, nvc = NC // LANES, NCC // LANES
-    lch, pch = levels // 2, pairs // 2
+    lch = levels // 2
     RQ, RQC = RF // groups, RC // groups
     s_f, s_c = math.sqrt(pair_all - 1), math.sqrt(level_all - 1)
 
@@ -215,65 +238,78 @@
     for load in loads[:nvc]:
         load.wait()
 
-    def place_level(m, _):
-        for r in range(RC):
-            row = jnp.concatenate([zv[v, pl.ds(m * K * RC + r, K, stride=RC), :] for v in range(nvc)], 1)
-            cq[m // 2, lax.rem(m, 2), HALO + r] = row
+    def columns_in(width):
+        shape = (width, width)
+        held = column_at(iota(shape, 1), width // LANES)
+        return jnp.where(iota(shape, 0) == held, 1.0, 0.0).astype(BF16)
+
+    order_c = columns_in(NCC)
+
+    def place_level(ch, _):
+        rows = []
+        for m in range(2):
+            for r in range(RC):
+                first = (2 * ch + m) * K * RC + r
+                rows.append(jnp.concatenate([zv[v, pl.ds(first, K, stride=RC), :] for v in range(nvc)], 1))
+        placed = select_dot(jnp.concatenate(rows, 0), order_c).reshape(2, RC, K, NCC)
+        for m in range(2):
+            cq[2 * ch + m, HALO : HALO + RC] = placed[m]
         return 0
 
-    lax.fori_loop(0, levels, place_level, 0)
+    lax.fori_loop(0, lch, place_level, 0)
     pl.semaphore_wait(barrier, len(targets))
 
-    def coarse_halo(ch, way):
-        src = HALO if way == 0 else RC
-        dst = HALO + RC if way == 0 else 0
+    def halo_copy(ref, lead, src, dst, rows, number, way):
         return pltpu.make_async_remote_copy(
-            src_ref=cq.at[ch, :, pl.ds(src, HALO)],
-            dst_ref=cq.at[ch, :, pl.ds(dst, HALO)],
-            send_sem=hs_sem.at[ch, way],
-            recv_sem=hr_sem.at[ch, way],
+            src_ref=ref.at[lead, pl.ds(src, rows)],
+            dst_ref=ref.at[lead, pl.ds(dst, rows)],
+            send_sem=hs_sem.at[number, way],
+            recv_sem=hr_sem.at[number, way],
             device_id=at(up if way == 0 else down, me),
             device_id_type=MESH,
         )
 
+    def level_halo(ch, way):
+        src, dst = ((HALO, HALO + RC), (RC, 0))[way]
+        return halo_copy(cq, pl.ds(2 * ch, 2), src, dst, HALO, ch, way)
+
     def fine_halo(j, way):
-        src = HALO if way == 0 else RF
-        dst = HALO + RF if way == 0 else 0
-        return pltpu.make_async_remote_copy(
-            src_ref=fq.at[j, pl.ds(src, HALO)],
-            dst_ref=fq.at[j, pl.ds(dst, HALO)],
-            send_sem=hs_sem.at[lch + pch + j, way],
-            recv_sem=hr_sem.at[lch + pch + j, way],
-            device_id=at(up if way == 0 else down, me),
-            device_id_type=MESH,
-        )
+        src, dst = ((HALO, HALO + RF), (RF, 0))[way]
+        return halo_copy(fq, j, src, dst, HALO, lch + j, way)
+
+    near = HALO // 2
+
+    def pair_halo(j, way):
+        src, dst = ((HALO + near, HALO + RC + near), (RC, 0))[way]
+        return halo_copy(cq, levels + j, src, dst, HALO - near, lch + pairs + j, way)
 
     for ch in range(lch):
         for way in range(2):
-            coarse_halo(ch, way).start()
+            level_halo(ch, way).start()
 
     for load in loads[nvc:]:
         load.wait()
 
-    halve = jnp.where(iota((NC, NCC), 0) // 2 == iota((NC, NCC), 1), 0.25, 0.0).astype(BF16)
-    widen = jnp.where(iota((NCC, NC), 1) // 2 == iota((NCC, NC), 0), 1.0, 0.0).astype(BF16)
+    order_f = columns_in(NC)
 
     def place_fine(m, _):
+        rows = []
         for r in range(RF):
-            row = jnp.concatenate([xv[v, pl.ds(m * K * RF + r, K, stride=RF), :] for v in range(nv)], 1)
-            fq[m, HALO + r] = row
-        own = fq[m, HALO : HALO + RF].reshape(RC, 2, K, NC)
-        rows = (own[:, 0] + own[:, 1]).reshape(RC * K, NC)
-        cq[lch + m // 2, lax.rem(m, 2), HALO : HALO + RC] = select_dot(rows, halve).reshape(RC, K, NCC)
+            first = m * K * RF + r
+            rows.append(jnp.concatenate([xv[v, pl.ds(first, K, stride=RF), :] for v in range(nv)], 1))
+        fq[m, HALO : HALO + RF] = select_dot(jnp.concatenate(rows, 0), order_f).reshape(RF, K, NC)
+        restrict(m, HALO, HALO, RC)
+        for way in range(2):
+            fine_halo(m, way).start()
+            pair_halo(m, way).start()
         return 0
 
+    def restrict(m, fine_row, coarse_row, count):
+        for r in range(count):
+            both = fq[m, fine_row + 2 * r] + fq[m, fine_row + 2 * r + 1]
+            cq[levels + m, coarse_row + r] = 0.25 * halved(both)
+
     lax.fori_loop(0, pairs, place_fine, 0)
-    for ch in range(lch, lch + pch):
-        for way in range(2):
-            coarse_halo(ch, way).start()
-    for j in range(pairs):
-        for way in range(2):
-            fine_halo(j, way).start()
 
     for small in smalls:
         small.wait()
@@ -288,8 +324,8 @@
         col = row_of(col_ref, b * sub, sub)
         lay = row_of(layer_ref, b * sub, sub)
         loc = row_of(row_ref, b * sub, sub) - tile * RF
-        oc[b] = jnp.where(iota((NC, per), 0) == col, 1.0, 0.0).astype(BF16)
-        occ[b] = jnp.where(iota((NCC, per), 0) == (col >> 1), 1.0, 0.0).astype(BF16)
+        oc[b] = jnp.where(iota((NC, per), 0) == place_of(col, nv), 1.0, 0.0).astype(BF16)
+        occ[b] = jnp.where(iota((NCC, per), 0) == place_of(col >> 1, nvc), 1.0, 0.0).astype(BF16)
         rm[b] = jnp.where(iota((RF * K, per), 0) == loc * K + lay, 1.0, 0.0).astype(F32)
         rmc[b] = jnp.where(iota((RC * K, per), 0) == (loc >> 1) * K + lay, 1.0, 0.0).astype(F32)
 
@@ -315,35 +351,41 @@
     row_c = tile * RC - HALO
     grid_c = tiles * RC
 
-    def coarse_chunk(ch, _):
-        coarse_halo(ch, 0).wait_recv()
-        coarse_halo(ch, 1).wait_recv()
+    def reader(ref, lead):
+        return lambda j: ref[lead + (j,)]
+
+    def writer(ref, lead):
+        def write(i, value):
+            ref[lead + (i,)] = value
+        return write
+
+    def coarse_steps(members):
+        count = len(members)
+        reads = [reader(cq, (m,)) for m in members]
+        ones = [(ct1, (m,)) for m in range(count)]
+        twos = [(ct2, (m,)) for m in range(count)]
+        ends = [writer(cres, (m,)) for m in members]
+        advance(reads, [writer(*x) for x in ones], RC + 8, row_c, grid_c, coarse_coef)
+        advance([reader(*x) for x in ones], [writer(*x) for x in twos], RC + 4, row_c + 2, grid_c, coarse_coef)
+        advance([reader(*x) for x in twos], ends, RC, row_c + 4, grid_c, coarse_coef)
+
+    def level_chunk(ch, _):
+        level_halo(ch, 0).wait_recv()
+        level_halo(ch, 1).wait_recv()
 
         def clear(first):
-            cq[ch, :, first : first + HALO] = jnp.zeros((2, HALO, K, NCC), F32)
+            cq[pl.ds(2 * ch, 2), first : first + HALO] = jnp.zeros((2, HALO, K, NCC), F32)
 
         zero_edges(lambda: clear(0), lambda: clear(HALO + RC))
-
-        def reader(ref, m, lead):
-            return lambda j: ref[lead + (m, j)]
-
-        def writer(ref, m, lead):
-            def write(i, value):
-                ref[lead + (m, i)] = value
-            return write
-
-        both = range(2)
-        advance([reader(cq, m, (ch,)) for m in both], [writer(ct1, m, ()) for m in both], RC + 8, row_c, grid_c, coarse_coef)
-        advance([reader(ct1, m, ()) for m in both], [writer(ct2, m, ()) for m in both], RC + 4, row_c + 2, grid_c, coarse_coef)
-        advance([reader(ct2, m, ()) for m in both], [writer(cres, m, (ch,)) for m in both], RC, row_c + 4, grid_c, coarse_coef)
+        coarse_steps([2 * ch, 2 * ch + 1])
         return 0
 
-    lax.fori_loop(0, lch + pch, coarse_chunk, 0)
+    lax.fori_loop(0, lch, level_chunk, 0)
 
     def level_send(i):
         peer = mem_peer(i)
         return pltpu.make_async_remote_copy(
-            src_ref=cres.at[pl.ds(0, lch), :, pl.ds(peer * RQC, RQC)],
+            src_ref=cres.at[pl.ds(0, levels), pl.ds(peer * RQC, RQC)],
             dst_ref=za.at[me],
             send_sem=ts_sem.at[0, i - 1],
             recv_sem=tr_sem.at[0, i - 1],
@@ -354,7 +396,7 @@
     def pair_send(i):
         peer = mem_peer(i)
         return pltpu.make_async_remote_copy(
-            src_ref=g.at[:, pl.ds(peer * RQ, RQ)],
+            src_ref=gn.at[:, pl.ds(peer * RQ, RQ)],
             dst_ref=ga.at[me],
             send_sem=ts_sem.at[1, i - 1],
             recv_sem=tr_sem.at[1, i - 1],
@@ -370,44 +412,43 @@
     grid_f = tiles * RF
 
     def fine_member(j, _):
-        fine_halo(j, 0).wait_recv()
-        fine_halo(j, 1).wait_recv()
-
-        def clear(first):
+        for way in range(2):
+            fine_halo(j, way).wait_recv()
+            pair_halo(j, way).wait_recv()
+
+        def clear(first, first_c):
             fq[j, first : first + HALO] = jnp.zeros((HALO, K, NC), F32)
-
-        zero_edges(lambda: clear(0), lambda: clear(HALO + RF))
-
-        def put(ref):
-            def write(i, value):
-                ref[i] = value
-            return write
+            cq[levels + j, first_c : first_c + HALO] = jnp.zeros((HALO, K, NCC), F32)
+
+        restrict(j, 0, near, near)
+        restrict(j, HALO + RF, HALO + RC, near)
+        zero_edges(lambda: clear(0, 0), lambda: clear(HALO + RF, HALO + RC))
+        coarse_steps([levels + j])
 
         def put_g(i, value):
-            g[j, i] = value
-
-        advance([lambda i: fq[j, i]], [put(ft1)], RF + 8, row_f, grid_f, fine_coef)
-        advance([lambda i: ft1[i]], [put(ft2)], RF + 4, row_f + 2, grid_f, fine_coef)
-        advance([lambda i: ft2[i]], [put_g], RF, row_f + 4, grid_f, fine_coef)
-        coarse = cres[lch + j // 2, lax.rem(j, 2)].reshape(RC * K, NCC)
-        wide = select_dot(coarse, widen).reshape(RC, 1, K, NC)
-        g[j] = (g[j].reshape(RC, 2, K, NC) - wide).reshape(RF, K, NC)
+            g[j, i] = value - doubled(cres[levels + j, i // 2])
+
+        advance([reader(fq, (j,))], [writer(ft1, ())], RF + 8, row_f, grid_f, fine_coef)
+        advance([reader(ft1, ())], [writer(ft2, ())], RF + 4, row_f + 2, grid_f, fine_coef)
+        advance([reader(ft2, ())], [put_g], RF, row_f + 4, grid_f, fine_coef)
         return 0
 
     lax.fori_loop(0, pairs, fine_member, 0)
 
-    def gather_block(b, _):
-        high, low = halves(cres[0:lch].reshape(levels * RC * K, NCC))
-        got = (dot(high, occ[b]) + dot(low, occ[b])).reshape(levels, RC * K, per)
-        z = jnp.sum(got * rmc[b][None], axis=1)
-        high, low = halves(g[...].reshape(pairs * RF * K, NC))
-        got = (dot(high, oc[b]) + dot(low, oc[b])).reshape(pairs, RF * K, per)
-        f = jnp.sum(got * rm[b][None], axis=1)
-        rest = sown.shape[1] - levels - pairs
-        sown[b] = jnp.concatenate([z, f, jnp.zeros((rest, per), F32)], 0)
+    def gather_block(pair, _):
+        fs = []
+        for part in range(2):
+            b = 2 * pair + part
+            high, low = halves(cres[0:levels].reshape(levels * RC * K, NCC))
+            got = (dot(high, occ[b]) + dot(low, occ[b])).reshape(levels, RC * K, per)
+            sown[b] = jnp.sum(got * rmc[b][None], axis=1)
+            high, low = halves(g[...].reshape(pairs * RF * K, NC))
+            got = (dot(high, oc[b]) + dot(low, oc[b])).reshape(pairs, RF * K, per)
+            fs.append(jnp.sum(got * rm[b][None], axis=1))
+        sown[nb + pair] = jnp.concatenate(fs, 0)
         return 0
 
-    lax.fori_loop(0, nb, gather_block, 0)
+    lax.fori_loop(0, nb // 2, gather_block, 0)
 
     def obs_send(i):
         return pltpu.make_async_remote_copy(
@@ -421,20 +462,32 @@
 
     for i in range(1, groups):
         obs_send(i).start()
+    sx[me] = sown[...]
+
+    def order_pair(j, _):
+        gn[j] = select_dot(g[j].reshape(RF * K, NC), columns_out(NC, 1)).reshape(RF, K, NC)
+        return 0
+
+    def columns_out(width, repeat):
+        shape = (width, width * repeat)
+        held = column_at(iota(shape, 0), width // LANES)
+        return jnp.where(held == iota(shape, 1) // repeat, 1.0, 0.0).astype(BF16)
+
+    lax.fori_loop(0, pairs, order_pair, 0)
+    for i in range(1, groups):
+        obs_send(i).wait_recv()
     for i in range(1, groups):
         pair_send(i).start()
-    sx[me] = sown[...]
-    own_level = pltpu.make_async_copy(cres.at[pl.ds(0, lch), :, pl.ds(me * RQC, RQC)], za.at[me], own_sem.at[0])
-    own_pair = pltpu.make_async_copy(g.at[:, pl.ds(me * RQ, RQ)], ga.at[me], own_sem.at[1])
+    own_level = pltpu.make_async_copy(cres.at[pl.ds(0, levels), pl.ds(me * RQC, RQC)], za.at[me], own_sem.at[0])
+    own_pair = pltpu.make_async_copy(gn.at[:, pl.ds(me * RQ, RQ)], ga.at[me], own_sem.at[1])
     own_level.start()
     own_pair.start()
-    for i in range(1, groups):
-        obs_send(i).wait_recv()
-
-    gram = jnp.zeros((E + 8, E), F32)
+
+    gram = jnp.zeros((E, E + 8), F32)
     for b in range(nb):
-        z = jnp.concatenate([sx[x, b, 0:levels] for x in range(groups)], 0)
-        f = jnp.concatenate([sx[x, b, levels : levels + pairs] for x in range(groups)], 0)
+        z = jnp.concatenate([sx[x, b] for x in range(groups)], 0)
+        first = (b % 2) * pairs
+        f = jnp.concatenate([sx[x, nb + b // 2, first : first + pairs] for x in range(groups)], 0)
         z_mean = jnp.mean(z, axis=0, keepdims=True)
         f_mean = jnp.mean(f, axis=0, keepdims=True)
         s = jnp.concatenate([(z - z_mean) * (1.0 / s_c), (f - f_mean) * (1.0 / s_f)], 0)
@@ -442,11 +495,13 @@
         slot = iota((1, per), 1) + b * per
         weight = jnp.where(slot < count_ref[0], 1.0 / row_of(var_ref, b * sub, sub), 0.0)
         extra = jnp.where(iota((8, per), 0) == 0, weight * innov, 0.0)
-        left = jnp.concatenate([s * weight, extra], 0)
+        right = jnp.concatenate([s * weight, extra], 0)
         gram = gram + lax.dot_general(
-            left, s, (((1,), (1,)), ((), ())), precision=HIGHEST, preferred_element_type=F32
+            s, right, (((1,), (1,)), ((), ())), precision=HIGHEST, preferred_element_type=F32
         )
-    gram = jnp.concatenate([gram, jnp.zeros((E + 8, LANES - E), F32)], 1)
+    half_e, half_l = E // 2, LANES // 2
+    gram = jnp.concatenate([gram, jnp.zeros((E, LANES - E - 8), F32)], 1)
+    gram = gram[:half_e] + pltpu.roll(gram[half_e:], half_l, axis=1)
 
     zk = level_all * K
 
@@ -455,8 +510,10 @@
         for i in range(1, groups):
             level_send(i).wait_recv()
 
+        widen = columns_out(NCC, 2)
+
         def one(rc, _):
-            z = za[:, :, :, rc].reshape(level_all, K, NCC)
+            z = za[:, :, rc].reshape(level_all, K, NCC)
             z_mean = jnp.mean(z, axis=0)
             high, low = halves(((z - z_mean[None]) * (1.0 / s_c)).reshape(zk, NCC))
             high, low = dot(high, widen).astype(BF16), dot(low, widen).astype(BF16)
@@ -497,7 +554,11 @@
     rows_t = E + pair_all + 8
     lane = iota((rows_t, LANES), 1)
     eye = jnp.where(iota((E, LANES), 0) == iota((E, LANES), 1), 1.0, 0.0).astype(F32)
-    table = jnp.concatenate([gram[0:E] + eye, gram[level_all:E], gram[E:]], 0)
+    full = jnp.concatenate([gram, pltpu.roll(gram, half_l, axis=1)], 0)
+    rhs = jnp.sum(full[:, E : E + 1] * eye, axis=0, keepdims=True)
+    full = jnp.where(iota((E, LANES), 1) < E, full, 0.0)
+    rhs = jnp.where(iota((8, LANES), 0) == 0, rhs, 0.0)
+    table = jnp.concatenate([full + eye, full[level_all:E], rhs], 0)
     width = 4
     for k in range(0, E, width):
         block = range(width)
@@ -598,12 +659,12 @@
     own_out.start()
     own_mean.start()
 
-    for ch in range(lch + pch):
-        for way in range(2):
-            coarse_halo(ch, way).wait_send()
-    for j in range(pairs):
-        for way in range(2):
+    for way in range(2):
+        for ch in range(lch):
+            level_halo(ch, way).wait_send()
+        for j in range(pairs):
             fine_halo(j, way).wait_send()
+            pair_halo(j, way).wait_send()
     for i in range(1, groups):
         level_send(i).wait_send()
         pair_send(i).wait_send()
@@ -681,11 +742,9 @@
     nb = 4
     per = slots // nb
     RQ, RQC = RF // groups, RC // groups
-    lch, pch = levels // 2, pairs // 2
-    chunks = lch + pch + pairs
+    chunks = levels // 2 + 2 * pairs
     peers = sum(size - 1 for _, size in stages)
     nv, nvc = NC // LANES, NCC // LANES
-    srows = -(-(levels + pairs) // 8) * 8
     anyspace = pl.BlockSpec(memory_space=pl.ANY)
     hbm = pl.BlockSpec(memory_space=pltpu.HBM)
     vmem = pl.BlockSpec(memory_space=pltpu.VMEM)
@@ -718,23 +777,24 @@
             pltpu.VMEM((nv, pairs * K * RF, LANES), F32),
             pltpu.VMEM((nvc, levels * K * RC, LANES), F32),
             pltpu.VMEM((pairs, RF + 2 * HALO, K, NC), F32),
-            pltpu.VMEM((lch + pch, 2, RC + 2 * HALO, K, NCC), F32),
+            pltpu.VMEM((levels + pairs, RC + 2 * HALO, K, NCC), F32),
             pltpu.VMEM((RF + 8, K, NC), F32),
             pltpu.VMEM((RF + 4, K, NC), F32),
             pltpu.VMEM((2, RC + 8, K, NCC), F32),
             pltpu.VMEM((2, RC + 4, K, NCC), F32),
-            pltpu.VMEM((lch + pch, 2, RC, K, NCC), F32),
+            pltpu.VMEM((levels + pairs, RC, K, NCC), F32),
+            pltpu.VMEM((pairs, RF, K, NC), F32),
             pltpu.VMEM((pairs, RF, K, NC), F32),
             pltpu.VMEM((groups, pairs, RQ, K, NC), F32),
-            pltpu.VMEM((groups, lch, 2, RQC, K, NCC), F32),
+            pltpu.VMEM((groups, levels, RQC, K, NCC), F32),
             pltpu.VMEM((nb, NC, per), BF16),
             pltpu.VMEM((nb, RF * K, per), F32),
             pltpu.VMEM((nb, NCC, per), BF16),
             pltpu.VMEM((nb, RC * K, per), F32),
-            pltpu.VMEM((nb, srows, per), F32),
-            pltpu.VMEM((groups, nb, srows, per), F32),
-            pltpu.VMEM((len(stages), E + 8, LANES), F32),
-            pltpu.VMEM((peers, E + 8, LANES), F32),
+            pltpu.VMEM((nb + nb // 2, levels, per), F32),
+            pltpu.VMEM((groups, nb + nb // 2, levels, per), F32),
+            pltpu.VMEM((len(stages), E // 2, LANES), F32),
+            pltpu.VMEM((peers, E // 2, LANES), F32),
             pltpu.VMEM((2 * (pairs * groups + 2) * K, E * K), BF16),
             pltpu.VMEM((2 * (pairs * groups + 2) * K, NC), F32),
             pltpu.VMEM((RQ, pairs * groups * K, NC), F32),

time: 74.6 us -> 59.8 us (0.80)
  the two profiles are of different devices: /device:TPU:0 before, /device:TPU:9 now
where the time goes in v3:
time: 59.8 us; the launch traced here: 59.7 us
  Pallas kernels  58.4 us (98%)
  between operations  1.29 us (2%)
    pallas_call x1, Pallas kernels, per_device(): pl.pallas_call(functools.partial(cycle_kernel, sizes), out_shape=(jax.Sha...  57 us
    pallas_call x1, Pallas kernels, per_device(): pl.pallas_call(functools.partial(order_kernel, K, RF), out_shape=(jax.Sha...  1.42 us

profile of v3, /device:TPU:9, one launch (start us, length us, event | category | flops | bytes accessed | tf_op | source)
XLA Modules:
  0.0 59.7 jit_solution(3345211646402078513)
XLA Ops:
  1.3 57.0 %cycle.1 = (f32[4,16,8,512]{3,2,1,0:T(8,128)S(1)}, f32[16,8,512]{2,1,0:T(8,128)S(1)}) custom-call(f32[512,512]{1,0:T(8,128)} %bitcast.9, f32[512,256]{1,0:T(8,128)} %bitcast.10, f32[8]{0:T(128)} %diff_in.1, f32[8]{0:T(128)} %hyper_in.1, f32[8]{0:T(128)} %drift_in.1, f32[8,128]{1,0:T(8,128)} %bitcast.11, f32[8,128]{1,0:T(8,128)} %bitcast.12, ...), custom_call_target="tpu_custom_call" | custom-call | tf_op jit(solution)/shard_map/cycle/pallas_call | solution.py:759
  58.3 1.4 %order.1 = (f32[512,512]{1,0:T(8,128)}, f32[128,512]{1,0:T(8,128)}) custom-call(f32[4,16,8,512]{3,2,1,0:T(8,128)S(1)} %get-tuple-element.6.pair_in, f32[16,8,512]{2,1,0:T(8,128)S(1)} %get-tuple-element.7.mean_in), custom_call_target="tpu_custom_call" | custom-call | tf_op jit(solution)/shard_map/order/pallas_call | solution.py:837

commit v4 on v3

--- a/solution.py
+++ b/solution.py
@@ -1,4 +1,5 @@
 import functools
+import itertools
 import math
 
 import jax
@@ -9,6 +10,7 @@
 from jax.sharding import PartitionSpec as P
 
 STEPS = 3
+EARLY = 4
 HALO = 2 * STEPS
 LANES = 128
 MESH = pl.DeviceIdType.MESH
@@ -75,27 +77,30 @@
     return out
 
 
-def advance(reads, writes, count, first_row, grid_rows, coef):
+def advance(reads, writes, count, first_row, grid_rows, own, coef):
     lap_c, hyp_c, drift_c, up_c, low_c = coef
     layers = up_c.shape[0]
-
-    def inside(j):
+    beside = (count + 4 - own) // 2
+
+    def inside(j, value):
+        if beside <= j < beside + own:
+            return value
         at = first_row + j
-        return jnp.where((at >= 0) & (at < grid_rows), 1.0, 0.0).astype(F32)
+        return value * jnp.where((at >= 0) & (at < grid_rows), 1.0, 0.0).astype(F32)
 
     def start(read):
         q0, q1, q2, q3 = read(0), read(1), read(2), read(3)
         left, right = shifted(q1)
-        f1 = (q2 + q0 + left + right - 4.0 * q1) * inside(1)
+        f1 = inside(1, q2 + q0 + left + right - 4.0 * q1)
         left, right = shifted(q2)
-        f2 = (q3 + q1 + left + right - 4.0 * q2) * inside(2)
+        f2 = inside(2, q3 + q1 + left + right - 4.0 * q2)
         return f1, f2, right - left
 
     def one(i, carry, read, write):
         f1, f2, side = carry
         q2, q3, q4 = read(i + 2), read(i + 3), read(i + 4)
         left, right = shifted(q3)
-        f3 = (q4 + q2 + left + right - 4.0 * q3) * inside(i + 3)
+        f3 = inside(i + 3, q4 + q2 + left + right - 4.0 * q3)
         fl, fr = shifted(f2)
         out = (
             0.8 * q2
@@ -105,7 +110,7 @@
             - hyp_c * (f1 + f3 + fl + fr)
             - drift_c * side
         )
-        write(i, out * inside(i + 2))
+        write(i, inside(i + 2, out))
         return f2, f3, right - left
 
     carries = [start(read) for read in reads]
@@ -148,7 +153,6 @@
     ct2,
     cres,
     g,
-    gn,
     ga,
     za,
     oc,
@@ -197,19 +201,25 @@
     def mem_peer(i):
         return lax.rem(me + i, groups)
 
-    def stage_peer(stage, i):
-        stride, size = stage
-        mine = lax.rem(tile // stride, size)
-        return tile + (lax.rem(mine + i, size) - mine) * stride
+    def stage_peers(stage):
+        peers = []
+        for offsets in itertools.product(*[range(size) for _, size in stage]):
+            if any(offsets):
+                peer = tile
+                for offset, (stride, size) in zip(offsets, stage):
+                    mine = lax.rem(tile // stride, size)
+                    peer = peer + (lax.rem(mine + offset, size) - mine) * stride
+                peers.append(peer)
+        return peers
 
     up = lax.rem(tile + tiles - 1, tiles)
     down = lax.rem(tile + 1, tiles)
 
     loads = []
+    for v in range(nv):
+        loads.append(pltpu.make_async_copy(fine_in.at[:, pl.ds(v * LANES, LANES)], xv.at[v], load_sem.at[v]))
     for v in range(nvc):
-        loads.append(pltpu.make_async_copy(coarse_in.at[:, pl.ds(v * LANES, LANES)], zv.at[v], load_sem.at[v]))
-    for v in range(nv):
-        loads.append(pltpu.make_async_copy(fine_in.at[:, pl.ds(v * LANES, LANES)], xv.at[v], load_sem.at[nvc + v]))
+        loads.append(pltpu.make_async_copy(coarse_in.at[:, pl.ds(v * LANES, LANES)], zv.at[v], load_sem.at[nv + v]))
     for load in loads:
         load.start()
     smalls = [
@@ -230,19 +240,74 @@
     targets = [(up, me), (down, me)]
     targets += [(tile, mem_peer(i)) for i in range(1, groups)]
     for stage in stages:
-        targets += [(stage_peer(stage, i), me) for i in range(1, stage[1])]
+        targets += [(peer, me) for peer in stage_peers(stage)]
     barrier = pltpu.get_barrier_semaphore()
     for target in targets:
         pl.semaphore_signal(barrier, inc=1, device_id=at(*target), device_id_type=MESH)
-
-    for load in loads[:nvc]:
-        load.wait()
 
     def columns_in(width):
         shape = (width, width)
         held = column_at(iota(shape, 1), width // LANES)
         return jnp.where(iota(shape, 0) == held, 1.0, 0.0).astype(BF16)
 
+    def halo_copy(ref, lead, src, dst, rows, number, way):
+        return pltpu.make_async_remote_copy(
+            src_ref=ref.at[lead, pl.ds(src, rows)],
+            dst_ref=ref.at[lead, pl.ds(dst, rows)],
+            send_sem=hs_sem.at[number, way],
+            recv_sem=hr_sem.at[number, way],
+            device_id=at(up if way == 0 else down, me),
+            device_id_type=MESH,
+        )
+
+    def level_halo(ch, way):
+        src, dst = ((HALO, HALO + RC), (RC, 0))[way]
+        return halo_copy(cq, pl.ds(2 * ch, 2), src, dst, HALO, ch, way)
+
+    def fine_halo(j, way):
+        src, dst = ((HALO, HALO + RF), (RF, 0))[way]
+        return halo_copy(fq, j, src, dst, HALO, lch + j, way)
+
+    near = HALO // 2
+
+    def pair_halo(j, way):
+        src, dst = ((HALO + near, HALO + RC + near), (RC, 0))[way]
+        return halo_copy(cq, levels + j, src, dst, HALO - near, lch + pairs + j, way)
+
+    order_f = columns_in(NC)
+
+    def place_fine(m):
+        rows = []
+        for r in range(RF):
+            first = m * K * RF + r
+            rows.append(jnp.concatenate([xv[v, pl.ds(first, K, stride=RF), :] for v in range(nv)], 1))
+        fq[m, HALO : HALO + RF] = select_dot(jnp.concatenate(rows, 0), order_f).reshape(RF, K, NC)
+        restrict(m, HALO, HALO, RC)
+
+    def send_fine(m):
+        for way in range(2):
+            fine_halo(m, way).start()
+            pair_halo(m, way).start()
+
+    def restrict(m, fine_row, coarse_row, count):
+        for r in range(count):
+            both = fq[m, fine_row + 2 * r] + fq[m, fine_row + 2 * r + 1]
+            cq[levels + m, coarse_row + r] = 0.25 * halved(both)
+
+    def place_and_send(m, _):
+        place_fine(m)
+        send_fine(m)
+        return 0
+
+    for load in loads[:nv]:
+        load.wait()
+    place_fine(0)
+    pl.semaphore_wait(barrier, len(targets))
+    send_fine(0)
+    lax.fori_loop(1, pairs, place_and_send, 0)
+
+    for load in loads[nv:]:
+        load.wait()
     order_c = columns_in(NCC)
 
     def place_level(ch, _):
@@ -254,62 +319,11 @@
         placed = select_dot(jnp.concatenate(rows, 0), order_c).reshape(2, RC, K, NCC)
         for m in range(2):
             cq[2 * ch + m, HALO : HALO + RC] = placed[m]
-        return 0
-
-    lax.fori_loop(0, lch, place_level, 0)
-    pl.semaphore_wait(barrier, len(targets))
-
-    def halo_copy(ref, lead, src, dst, rows, number, way):
-        return pltpu.make_async_remote_copy(
-            src_ref=ref.at[lead, pl.ds(src, rows)],
-            dst_ref=ref.at[lead, pl.ds(dst, rows)],
-            send_sem=hs_sem.at[number, way],
-            recv_sem=hr_sem.at[number, way],
-            device_id=at(up if way == 0 else down, me),
-            device_id_type=MESH,
-        )
-
-    def level_halo(ch, way):
-        src, dst = ((HALO, HALO + RC), (RC, 0))[way]
-        return halo_copy(cq, pl.ds(2 * ch, 2), src, dst, HALO, ch, way)
-
-    def fine_halo(j, way):
-        src, dst = ((HALO, HALO + RF), (RF, 0))[way]
-        return halo_copy(fq, j, src, dst, HALO, lch + j, way)
-
-    near = HALO // 2
-
-    def pair_halo(j, way):
-        src, dst = ((HALO + near, HALO + RC + near), (RC, 0))[way]
-        return halo_copy(cq, levels + j, src, dst, HALO - near, lch + pairs + j, way)
-
-    for ch in range(lch):
         for way in range(2):
             level_halo(ch, way).start()
-
-    for load in loads[nvc:]:
-        load.wait()
-
-    order_f = columns_in(NC)
-
-    def place_fine(m, _):
-        rows = []
-        for r in range(RF):
-            first = m * K * RF + r
-            rows.append(jnp.concatenate([xv[v, pl.ds(first, K, stride=RF), :] for v in range(nv)], 1))
-        fq[m, HALO : HALO + RF] = select_dot(jnp.concatenate(rows, 0), order_f).reshape(RF, K, NC)
-        restrict(m, HALO, HALO, RC)
-        for way in range(2):
-            fine_halo(m, way).start()
-            pair_halo(m, way).start()
         return 0
 
-    def restrict(m, fine_row, coarse_row, count):
-        for r in range(count):
-            both = fq[m, fine_row + 2 * r] + fq[m, fine_row + 2 * r + 1]
-            cq[levels + m, coarse_row + r] = 0.25 * halved(both)
-
-    lax.fori_loop(0, pairs, place_fine, 0)
+    lax.fori_loop(0, lch, place_level, 0)
 
     for small in smalls:
         small.wait()
@@ -365,9 +379,31 @@
         ones = [(ct1, (m,)) for m in range(count)]
         twos = [(ct2, (m,)) for m in range(count)]
         ends = [writer(cres, (m,)) for m in members]
-        advance(reads, [writer(*x) for x in ones], RC + 8, row_c, grid_c, coarse_coef)
-        advance([reader(*x) for x in ones], [writer(*x) for x in twos], RC + 4, row_c + 2, grid_c, coarse_coef)
-        advance([reader(*x) for x in twos], ends, RC, row_c + 4, grid_c, coarse_coef)
+        advance(reads, [writer(*x) for x in ones], RC + 8, row_c, grid_c, RC, coarse_coef)
+        advance([reader(*x) for x in ones], [writer(*x) for x in twos], RC + 4, row_c + 2, grid_c, RC, coarse_coef)
+        advance([reader(*x) for x in twos], ends, RC, row_c + 4, grid_c, RC, coarse_coef)
+
+    def level_send(ch, i):
+        peer = mem_peer(i)
+        return pltpu.make_async_remote_copy(
+            src_ref=cres.at[pl.ds(2 * ch, 2), pl.ds(peer * RQC, RQC)],
+            dst_ref=za.at[me, pl.ds(2 * ch, 2)],
+            send_sem=ts_sem.at[ch, i - 1],
+            recv_sem=tr_sem.at[ch, i - 1],
+            device_id=at(tile, peer),
+            device_id_type=MESH,
+        )
+
+    def pair_send(j, i):
+        peer = mem_peer(i)
+        return pltpu.make_async_remote_copy(
+            src_ref=g.at[j, pl.ds(peer * RQ, RQ)],
+            dst_ref=ga.at[me, j],
+            send_sem=ts_sem.at[lch + j, i - 1],
+            recv_sem=tr_sem.at[lch + j, i - 1],
+            device_id=at(tile, peer),
+            device_id_type=MESH,
+        )
 
     def level_chunk(ch, _):
         level_halo(ch, 0).wait_recv()
@@ -380,32 +416,30 @@
         coarse_steps([2 * ch, 2 * ch + 1])
         return 0
 
-    lax.fori_loop(0, lch, level_chunk, 0)
-
-    def level_send(i):
-        peer = mem_peer(i)
+    def gather(values, columns, rows, number):
+        high, low = halves(values)
+        got = dot(high, columns) + dot(low, columns)
+        return jnp.sum(got.reshape((number,) + rows.shape) * rows[None], axis=1)
+
+    def level_gather(b, _):
+        sown[b] = gather(cres[0:levels].reshape(levels * RC * K, NCC), occ[b], rmc[b], levels)
+        return 0
+
+    def pair_gather(half, _):
+        fs = [gather(g[...].reshape(pairs * RF * K, NC), oc[2 * half + b], rm[2 * half + b], pairs) for b in range(2)]
+        sown[nb + half] = jnp.concatenate(fs, 0)
+        return 0
+
+    def obs_send(part, i):
+        span = (pl.ds(nb, nb // 2), pl.ds(0, nb))[part]
         return pltpu.make_async_remote_copy(
-            src_ref=cres.at[pl.ds(0, levels), pl.ds(peer * RQC, RQC)],
-            dst_ref=za.at[me],
-            send_sem=ts_sem.at[0, i - 1],
-            recv_sem=tr_sem.at[0, i - 1],
-            device_id=at(tile, peer),
+            src_ref=sown.at[span],
+            dst_ref=sx.at[me, span],
+            send_sem=ss_sem.at[part, i - 1],
+            recv_sem=sr_sem.at[part, i - 1],
+            device_id=at(tile, mem_peer(i)),
             device_id_type=MESH,
         )
-
-    def pair_send(i):
-        peer = mem_peer(i)
-        return pltpu.make_async_remote_copy(
-            src_ref=gn.at[:, pl.ds(peer * RQ, RQ)],
-            dst_ref=ga.at[me],
-            send_sem=ts_sem.at[1, i - 1],
-            recv_sem=tr_sem.at[1, i - 1],
-            device_id=at(tile, peer),
-            device_id_type=MESH,
-        )
-
-    for i in range(1, groups):
-        level_send(i).start()
 
     fine_coef = coefs(1.0, 1.0, 1.0, NC)
     row_f = tile * RF - HALO
@@ -428,58 +462,39 @@
         def put_g(i, value):
             g[j, i] = value - doubled(cres[levels + j, i // 2])
 
-        advance([reader(fq, (j,))], [writer(ft1, ())], RF + 8, row_f, grid_f, fine_coef)
-        advance([reader(ft1, ())], [writer(ft2, ())], RF + 4, row_f + 2, grid_f, fine_coef)
-        advance([reader(ft2, ())], [put_g], RF, row_f + 4, grid_f, fine_coef)
+        advance([reader(fq, (j,))], [writer(ft1, ())], RF + 8, row_f, grid_f, RF, fine_coef)
+        advance([reader(ft1, ())], [writer(ft2, ())], RF + 4, row_f + 2, grid_f, RF, fine_coef)
+        advance([reader(ft2, ())], [put_g], RF, row_f + 4, grid_f, RF, fine_coef)
+
+        @pl.when(j < EARLY)
+        def _():
+            for i in range(1, groups):
+                pair_send(j, i).start()
+
         return 0
 
     lax.fori_loop(0, pairs, fine_member, 0)
 
-    def gather_block(pair, _):
-        fs = []
-        for part in range(2):
-            b = 2 * pair + part
-            high, low = halves(cres[0:levels].reshape(levels * RC * K, NCC))
-            got = (dot(high, occ[b]) + dot(low, occ[b])).reshape(levels, RC * K, per)
-            sown[b] = jnp.sum(got * rmc[b][None], axis=1)
-            high, low = halves(g[...].reshape(pairs * RF * K, NC))
-            got = (dot(high, oc[b]) + dot(low, oc[b])).reshape(pairs, RF * K, per)
-            fs.append(jnp.sum(got * rm[b][None], axis=1))
-        sown[nb + pair] = jnp.concatenate(fs, 0)
-        return 0
-
-    lax.fori_loop(0, nb // 2, gather_block, 0)
-
-    def obs_send(i):
-        return pltpu.make_async_remote_copy(
-            src_ref=sown,
-            dst_ref=sx.at[me],
-            send_sem=ss_sem.at[i - 1],
-            recv_sem=sr_sem.at[i - 1],
-            device_id=at(tile, mem_peer(i)),
-            device_id_type=MESH,
-        )
-
+    lax.fori_loop(0, nb // 2, pair_gather, 0)
     for i in range(1, groups):
-        obs_send(i).start()
+        obs_send(0, i).start()
+
+    lax.fori_loop(0, lch, level_chunk, 0)
+    lax.fori_loop(0, nb, level_gather, 0)
+    for i in range(1, groups):
+        obs_send(1, i).start()
     sx[me] = sown[...]
-
-    def order_pair(j, _):
-        gn[j] = select_dot(g[j].reshape(RF * K, NC), columns_out(NC, 1)).reshape(RF, K, NC)
-        return 0
-
-    def columns_out(width, repeat):
-        shape = (width, width * repeat)
-        held = column_at(iota(shape, 0), width // LANES)
-        return jnp.where(held == iota(shape, 1) // repeat, 1.0, 0.0).astype(BF16)
-
-    lax.fori_loop(0, pairs, order_pair, 0)
     for i in range(1, groups):
-        obs_send(i).wait_recv()
-    for i in range(1, groups):
-        pair_send(i).start()
+        obs_send(0, i).wait_recv()
+        obs_send(1, i).wait_recv()
+    for j in range(EARLY, pairs):
+        for i in range(1, groups):
+            pair_send(j, i).start()
+    for ch in range(lch):
+        for i in range(1, groups):
+            level_send(ch, i).start()
     own_level = pltpu.make_async_copy(cres.at[pl.ds(0, levels), pl.ds(me * RQC, RQC)], za.at[me], own_sem.at[0])
-    own_pair = pltpu.make_async_copy(gn.at[:, pl.ds(me * RQ, RQ)], ga.at[me], own_sem.at[1])
+    own_pair = pltpu.make_async_copy(g.at[:, pl.ds(me * RQ, RQ)], ga.at[me], own_sem.at[1])
     own_level.start()
     own_pair.start()
 
@@ -507,8 +522,9 @@
 
     def level_anomalies():
         own_level.wait()
-        for i in range(1, groups):
-            level_send(i).wait_recv()
+        for ch in range(lch):
+            for i in range(1, groups):
+                level_send(ch, i).wait_recv()
 
         widen = columns_out(NCC, 2)
 
@@ -521,35 +537,65 @@
             for half in range(2):
                 dh[2 * rc + half, 0:zk] = high
                 dl[2 * rc + half, 0:zk] = low
-                mu[2 * rc + half] = wide_mean
+                mu[2 * rc + half] = mu[2 * rc + half] + wide_mean
             return 0
 
         lax.fori_loop(0, RQC, one, 0)
+
+    def columns_out(width, repeat):
+        shape = (width, width * repeat)
+        held = column_at(iota(shape, 0), width // LANES)
+        return jnp.where(held == iota(shape, 1) // repeat, 1.0, 0.0).astype(BF16)
+
+    def pair_anomalies():
+        own_pair.wait()
+        for j in range(pairs):
+            for i in range(1, groups):
+                pair_send(j, i).wait_recv()
+        natural = columns_out(NC, 1)
+
+        def one(r, _):
+            f = ga[:, :, r].reshape(pair_all, K, NC)
+            f_mean = jnp.mean(f, axis=0)
+            mu[r] = select_dot(f_mean, natural)
+            anom = ((f - f_mean[None]) * (1.0 / s_f)).reshape(pair_all * K, NC)
+            high = anom.astype(BF16)
+            rest = anom - high.astype(F32)
+            mid = rest.astype(BF16)
+            low = (rest - mid.astype(F32)).astype(BF16)
+            high, mid, low = dot(high, natural), dot(mid, natural), dot(low, natural)
+            dg[r] = high + (mid + low)
+            dh[r, zk:] = high.astype(BF16)
+            dl[r, zk:] = mid.astype(BF16)
+            return 0
+
+        lax.fori_loop(0, RQ, one, 0)
 
     slot0 = 0
     for s, stage in enumerate(stages):
         ar0[s] = gram
         sends = []
-        for i in range(1, stage[1]):
-            n = slot0 + i - 1
+        for n, peer in enumerate(stage_peers(stage), slot0):
             send = pltpu.make_async_remote_copy(
                 src_ref=ar0.at[s],
                 dst_ref=ar1.at[n],
                 send_sem=as_sem.at[n],
                 recv_sem=ar_sem.at[n],
-                device_id=at(stage_peer(stage, i), me),
+                device_id=at(peer, me),
                 device_id_type=MESH,
             )
             send.start()
             sends.append((send, n))
         if s == 0:
+            pair_anomalies()
+        if s == len(stages) - 1:
             level_anomalies()
         for send, n in sends:
             send.wait_recv()
             gram = gram + ar1[n]
         for send, n in sends:
             send.wait_send()
-        slot0 += stage[1] - 1
+        slot0 += len(sends)
 
     rows_t = E + pair_all + 8
     lane = iota((rows_t, LANES), 1)
@@ -603,23 +649,6 @@
     kron_ref[0:kron_rows] = kron(coef_h)
     kron_ref[kron_rows:] = kron(coef_l)
 
-    own_pair.wait()
-    for i in range(1, groups):
-        pair_send(i).wait_recv()
-
-    def pair_anomalies(r, _):
-        f = ga[:, :, r].reshape(pair_all, K, NC)
-        f_mean = jnp.mean(f, axis=0)
-        mu[r] = mu[r] + f_mean
-        anom = ((f - f_mean[None]) * (1.0 / s_f)).reshape(pair_all * K, NC)
-        dg[r] = anom
-        high, low = halves(anom)
-        dh[r, zk:] = high
-        dl[r, zk:] = low
-        return 0
-
-    lax.fori_loop(0, RQ, pair_anomalies, 0)
-
     def result_send(r, i):
         peer = mem_peer(i)
         pair_copy = pltpu.make_async_remote_copy(
@@ -648,7 +677,7 @@
         total = inc[0:kron_rows] + inc[kron_rows:] + more
         ob[:, r] = (s_f * (dg[r] + total[:np8])).reshape(pair_all, K, NC)
         mb[r] = mu[r] + total[np8 : np8 + K]
-        for i in range(1, groups):
+        for i in sorted(range(1, groups), key=lambda i: -min(i, groups - i)):
             for copy in result_send(r, i):
                 copy.start()
         return 0
@@ -666,9 +695,12 @@
             fine_halo(j, way).wait_send()
             pair_halo(j, way).wait_send()
     for i in range(1, groups):
-        level_send(i).wait_send()
-        pair_send(i).wait_send()
-        obs_send(i).wait_send()
+        for ch in range(lch):
+            level_send(ch, i).wait_send()
+        for j in range(pairs):
+            pair_send(j, i).wait_send()
+        for part in range(2):
+            obs_send(part, i).wait_send()
     own_out.wait()
     own_mean.wait()
     for r in range(RQ):
@@ -710,12 +742,12 @@
 
 
 def axis_stages(tiles):
-    stages, stride = [], 1
+    axes, stride = [], 1
     for size in (2, 4, 4):
         if stride < tiles:
-            stages.append((stride, size))
+            axes.append((stride, size))
             stride *= size
-    return tuple(stages)
+    return tuple(stage for stage in (tuple(axes[:2]), tuple(axes[2:])) if stage)
 
 
 def per_device(
@@ -743,7 +775,7 @@
     per = slots // nb
     RQ, RQC = RF // groups, RC // groups
     chunks = levels // 2 + 2 * pairs
-    peers = sum(size - 1 for _, size in stages)
+    peers = sum(math.prod(size for _, size in stage) - 1 for stage in stages)
     nv, nvc = NC // LANES, NCC // LANES
     anyspace = pl.BlockSpec(memory_space=pl.ANY)
     hbm = pl.BlockSpec(memory_space=pltpu.HBM)
@@ -784,7 +816,6 @@
             pltpu.VMEM((2, RC + 4, K, NCC), F32),
             pltpu.VMEM((levels + pairs, RC, K, NCC), F32),
             pltpu.VMEM((pairs, RF, K, NC), F32),
-            pltpu.VMEM((pairs, RF, K, NC), F32),
             pltpu.VMEM((groups, pairs, RQ, K, NC), F32),
             pltpu.VMEM((groups, levels, RQC, K, NCC), F32),
             pltpu.VMEM((nb, NC, per), BF16),
@@ -807,12 +838,12 @@
             dma((9,)),
             dma((chunks, 2)),
             dma((chunks, 2)),
-            dma((groups - 1,)),
-            dma((groups - 1,)),
+            dma((2, groups - 1)),
+            dma((2, groups - 1)),
             dma((peers,)),
             dma((peers,)),
-            dma((2, groups - 1)),
-            dma((2, groups - 1)),
+            dma((levels // 2 + pairs, groups - 1)),
+            dma((levels // 2 + pairs, groups - 1)),
             dma((2, RQ, groups - 1)),
             dma((2, RQ, groups - 1)),
             dma((4,)),

time: 59.8 us -> 58.4 us (0.977)
  the two profiles are of different devices: /device:TPU:9 before, /device:TPU:0 now
where the time goes in v4:
time: 58.4 us; the launch traced here: 57.7 us
  Pallas kernels  56.4 us (97%)
  between operations  1.29 us (2%)
    pallas_call x1, Pallas kernels, per_device(): pl.pallas_call(functools.partial(cycle_kernel, sizes), out_shape=(jax.Sha...  55 us
    pallas_call x1, Pallas kernels, per_device(): pl.pallas_call(functools.partial(order_kernel, K, RF), out_shape=(jax.Sha...  1.42 us

profile of v4, /device:TPU:0, one launch (start us, length us, event | category | flops | bytes accessed | tf_op | source)
XLA Modules:
  0.0 57.7 jit_solution(2773164495259624668)
XLA Ops:
  1.3 55.0 %cycle.1 = (f32[4,16,8,512]{3,2,1,0:T(8,128)S(1)}, f32[16,8,512]{2,1,0:T(8,128)S(1)}) custom-call(f32[512,512]{1,0:T(8,128)} %bitcast.9, f32[512,256]{1,0:T(8,128)} %bitcast.10, f32[8]{0:T(128)} %diff_in.1, f32[8]{0:T(128)} %hyper_in.1, f32[8]{0:T(128)} %drift_in.1, f32[8,128]{1,0:T(8,128)} %bitcast.11, f32[8,128]{1,0:T(8,128)} %bitcast.12, ...), custom_call_target="tpu_custom_call" | custom-call | tf_op jit(solution)/shard_map/cycle/pallas_call | solution.py:791
  56.3 1.4 %order.1 = (f32[512,512]{1,0:T(8,128)}, f32[128,512]{1,0:T(8,128)}) custom-call(f32[4,16,8,512]{3,2,1,0:T(8,128)S(1)} %get-tuple-element.6.pair_in, f32[16,8,512]{2,1,0:T(8,128)S(1)} %get-tuple-element.7.mean_in), custom_call_target="tpu_custom_call" | custom-call | tf_op jit(solution)/shard_map/order/pallas_call | solution.py:868

commit v5 on v4

--- a/solution.py
+++ b/solution.py
@@ -10,7 +10,7 @@
 from jax.sharding import PartitionSpec as P
 
 STEPS = 3
-EARLY = 4
+EARLY = 1
 HALO = 2 * STEPS
 LANES = 128
 MESH = pl.DeviceIdType.MESH
@@ -51,11 +51,11 @@
     return (column & (parts - 1)) * LANES + (column >> shift)
 
 
-def shifted(row):
+def shifted(row, packed):
     width = row.shape[-1]
     first, last = row[:, :LANES], row[:, width - LANES :]
-    left = jnp.concatenate([pltpu.roll(last, 1, axis=1), row[:, : width - LANES]], 1)
-    right = jnp.concatenate([row[:, LANES:], pltpu.roll(first, LANES - 1, axis=1)], 1)
+    left = jnp.concatenate([pltpu.roll(last, packed, axis=1), row[:, : width - LANES]], 1)
+    right = jnp.concatenate([row[:, LANES:], pltpu.roll(first, LANES - packed, axis=1)], 1)
     return left, right
 
 
@@ -77,7 +77,7 @@
     return out
 
 
-def advance(reads, writes, count, first_row, grid_rows, own, coef):
+def advance(read, write, count, first_row, grid_rows, own, coef, packed=1):
     lap_c, hyp_c, drift_c, up_c, low_c = coef
     layers = up_c.shape[0]
     beside = (count + 4 - own) // 2
@@ -88,20 +88,17 @@
         at = first_row + j
         return value * jnp.where((at >= 0) & (at < grid_rows), 1.0, 0.0).astype(F32)
 
-    def start(read):
-        q0, q1, q2, q3 = read(0), read(1), read(2), read(3)
-        left, right = shifted(q1)
-        f1 = inside(1, q2 + q0 + left + right - 4.0 * q1)
-        left, right = shifted(q2)
-        f2 = inside(2, q3 + q1 + left + right - 4.0 * q2)
-        return f1, f2, right - left
-
-    def one(i, carry, read, write):
-        f1, f2, side = carry
+    q0, q1, q2, q3 = read(0), read(1), read(2), read(3)
+    left, right = shifted(q1, packed)
+    f1 = inside(1, q2 + q0 + left + right - 4.0 * q1)
+    left, right = shifted(q2, packed)
+    f2 = inside(2, q3 + q1 + left + right - 4.0 * q2)
+    side = right - left
+    for i in range(count):
         q2, q3, q4 = read(i + 2), read(i + 3), read(i + 4)
-        left, right = shifted(q3)
+        left, right = shifted(q3, packed)
         f3 = inside(i + 3, q4 + q2 + left + right - 4.0 * q3)
-        fl, fr = shifted(f2)
+        fl, fr = shifted(f2, packed)
         out = (
             0.8 * q2
             + up_c * pltpu.roll(q2, layers - 1, axis=0)
@@ -111,12 +108,7 @@
             - drift_c * side
         )
         write(i, inside(i + 2, out))
-        return f2, f3, right - left
-
-    carries = [start(read) for read in reads]
-    for i in range(count):
-        for m in range(len(reads)):
-            carries[m] = one(i, carries[m], reads[m], writes[m])
+        f1, f2, side = f2, f3, right - left
 
 
 def cycle_kernel(
@@ -147,12 +139,18 @@
     zv,
     fq,
     cq,
+    zq,
     ft1,
     ft2,
     ct1,
     ct2,
     cres,
+    zres,
     g,
+    gh,
+    gl,
+    zh,
+    zl,
     ga,
     za,
     oc,
@@ -216,10 +214,10 @@
     down = lax.rem(tile + 1, tiles)
 
     loads = []
+    for v in range(nvc):
+        loads.append(pltpu.make_async_copy(coarse_in.at[:, pl.ds(v * LANES, LANES)], zv.at[v], load_sem.at[v]))
     for v in range(nv):
-        loads.append(pltpu.make_async_copy(fine_in.at[:, pl.ds(v * LANES, LANES)], xv.at[v], load_sem.at[v]))
-    for v in range(nvc):
-        loads.append(pltpu.make_async_copy(coarse_in.at[:, pl.ds(v * LANES, LANES)], zv.at[v], load_sem.at[nv + v]))
+        loads.append(pltpu.make_async_copy(fine_in.at[:, pl.ds(v * LANES, LANES)], xv.at[v], load_sem.at[nvc + v]))
     for load in loads:
         load.start()
     smalls = [
@@ -262,7 +260,7 @@
 
     def level_halo(ch, way):
         src, dst = ((HALO, HALO + RC), (RC, 0))[way]
-        return halo_copy(cq, pl.ds(2 * ch, 2), src, dst, HALO, ch, way)
+        return halo_copy(zq, ch, src, dst, HALO, ch, way)
 
     def fine_halo(j, way):
         src, dst = ((HALO, HALO + RF), (RF, 0))[way]
@@ -272,7 +270,32 @@
 
     def pair_halo(j, way):
         src, dst = ((HALO + near, HALO + RC + near), (RC, 0))[way]
-        return halo_copy(cq, levels + j, src, dst, HALO - near, lch + pairs + j, way)
+        return halo_copy(cq, j, src, dst, HALO - near, lch + pairs + j, way)
+
+    def level_column(p):
+        return (p % LANES) // 2 * nv + p // LANES
+
+    p = iota((2 * NCC, NC), 1)
+    order_c = jnp.where(iota((2 * NCC, NC), 0) == p % 2 * NCC + level_column(p), 1.0, 0.0).astype(BF16)
+
+    def place_level(ch, _):
+        rows = []
+        for r in range(RC):
+            row = []
+            for m in range(2):
+                row += [zv[v, pl.ds((2 * ch + m) * K * RC + r, K, stride=RC), :] for v in range(nvc)]
+            rows.append(jnp.concatenate(row, 1))
+        zq[ch, HALO : HALO + RC] = select_dot(jnp.concatenate(rows, 0), order_c).reshape(RC, K, NC)
+        return 0
+
+    for load in loads[:nvc]:
+        load.wait()
+    lax.fori_loop(0, lch, place_level, 0)
+
+    pl.semaphore_wait(barrier, len(targets))
+    for ch in range(lch):
+        for way in range(2):
+            level_halo(ch, way).start()
 
     order_f = columns_in(NC)
 
@@ -292,38 +315,16 @@
     def restrict(m, fine_row, coarse_row, count):
         for r in range(count):
             both = fq[m, fine_row + 2 * r] + fq[m, fine_row + 2 * r + 1]
-            cq[levels + m, coarse_row + r] = 0.25 * halved(both)
+            cq[m, coarse_row + r] = 0.25 * halved(both)
 
     def place_and_send(m, _):
         place_fine(m)
         send_fine(m)
         return 0
 
-    for load in loads[:nv]:
+    for load in loads[nvc:]:
         load.wait()
-    place_fine(0)
-    pl.semaphore_wait(barrier, len(targets))
-    send_fine(0)
-    lax.fori_loop(1, pairs, place_and_send, 0)
-
-    for load in loads[nv:]:
-        load.wait()
-    order_c = columns_in(NCC)
-
-    def place_level(ch, _):
-        rows = []
-        for m in range(2):
-            for r in range(RC):
-                first = (2 * ch + m) * K * RC + r
-                rows.append(jnp.concatenate([zv[v, pl.ds(first, K, stride=RC), :] for v in range(nvc)], 1))
-        placed = select_dot(jnp.concatenate(rows, 0), order_c).reshape(2, RC, K, NCC)
-        for m in range(2):
-            cq[2 * ch + m, HALO : HALO + RC] = placed[m]
-        for way in range(2):
-            level_halo(ch, way).start()
-        return 0
-
-    lax.fori_loop(0, lch, place_level, 0)
+    lax.fori_loop(0, pairs, place_and_send, 0)
 
     for small in smalls:
         small.wait()
@@ -339,7 +340,9 @@
         lay = row_of(layer_ref, b * sub, sub)
         loc = row_of(row_ref, b * sub, sub) - tile * RF
         oc[b] = jnp.where(iota((NC, per), 0) == place_of(col, nv), 1.0, 0.0).astype(BF16)
-        occ[b] = jnp.where(iota((NCC, per), 0) == place_of(col >> 1, nvc), 1.0, 0.0).astype(BF16)
+        place = ((col >> 1) & (nv - 1)) * LANES + (col >> 1) // nv * 2
+        for m in range(2):
+            occ[b, m] = jnp.where(iota((NC, per), 0) == place + m, 1.0, 0.0).astype(BF16)
         rm[b] = jnp.where(iota((RF * K, per), 0) == loc * K + lay, 1.0, 0.0).astype(F32)
         rmc[b] = jnp.where(iota((RC * K, per), 0) == (loc >> 1) * K + lay, 1.0, 0.0).astype(F32)
 
@@ -362,6 +365,7 @@
             clear_high()
 
     coarse_coef = coefs(0.25, 0.0625, 0.5, NCC)
+    level_coef = coefs(0.25, 0.0625, 0.5, NC)
     row_c = tile * RC - HALO
     grid_c = tiles * RC
 
@@ -373,21 +377,22 @@
             ref[lead + (i,)] = value
         return write
 
-    def coarse_steps(members):
-        count = len(members)
-        reads = [reader(cq, (m,)) for m in members]
-        ones = [(ct1, (m,)) for m in range(count)]
-        twos = [(ct2, (m,)) for m in range(count)]
-        ends = [writer(cres, (m,)) for m in members]
-        advance(reads, [writer(*x) for x in ones], RC + 8, row_c, grid_c, RC, coarse_coef)
-        advance([reader(*x) for x in ones], [writer(*x) for x in twos], RC + 4, row_c + 2, grid_c, RC, coarse_coef)
-        advance([reader(*x) for x in twos], ends, RC, row_c + 4, grid_c, RC, coarse_coef)
+    def coarse_steps(j):
+        advance(reader(cq, (j,)), writer(ct1, ()), RC + 8, row_c, grid_c, RC, coarse_coef)
+        advance(reader(ct1, ()), writer(ct2, ()), RC + 4, row_c + 2, grid_c, RC, coarse_coef)
+        advance(reader(ct2, ()), writer(cres, (j,)), RC, row_c + 4, grid_c, RC, coarse_coef)
+
+    def level_steps(ch):
+        advance(reader(zq, (ch,)), writer(ft1, ()), RC + 8, row_c, grid_c, RC, level_coef, 2)
+        advance(reader(ft1, ()), writer(ft2, ()), RC + 4, row_c + 2, grid_c, RC, level_coef, 2)
+        advance(reader(ft2, ()), writer(zres, (ch,)), RC, row_c + 4, grid_c, RC, level_coef, 2)
+        zh[ch], zl[ch] = halves(zres[ch].reshape(RC * K, NC))
 
     def level_send(ch, i):
         peer = mem_peer(i)
         return pltpu.make_async_remote_copy(
-            src_ref=cres.at[pl.ds(2 * ch, 2), pl.ds(peer * RQC, RQC)],
-            dst_ref=za.at[me, pl.ds(2 * ch, 2)],
+            src_ref=zres.at[ch, pl.ds(peer * RQC, RQC)],
+            dst_ref=za.at[me, ch],
             send_sem=ts_sem.at[ch, i - 1],
             recv_sem=tr_sem.at[ch, i - 1],
             device_id=at(tile, peer),
@@ -410,24 +415,26 @@
         level_halo(ch, 1).wait_recv()
 
         def clear(first):
-            cq[pl.ds(2 * ch, 2), first : first + HALO] = jnp.zeros((2, HALO, K, NCC), F32)
+            zq[ch, first : first + HALO] = jnp.zeros((HALO, K, NC), F32)
 
         zero_edges(lambda: clear(0), lambda: clear(HALO + RC))
-        coarse_steps([2 * ch, 2 * ch + 1])
+        level_steps(ch)
+        for i in range(1, groups):
+            level_send(ch, i).start()
         return 0
 
-    def gather(values, columns, rows, number):
-        high, low = halves(values)
-        got = dot(high, columns) + dot(low, columns)
+    def gather(high, low, columns, rows):
+        number = high.shape[0]
+        flat = (number * high.shape[1], high.shape[2])
+        got = dot(high[...].reshape(flat), columns) + dot(low[...].reshape(flat), columns)
         return jnp.sum(got.reshape((number,) + rows.shape) * rows[None], axis=1)
 
     def level_gather(b, _):
-        sown[b] = gather(cres[0:levels].reshape(levels * RC * K, NCC), occ[b], rmc[b], levels)
+        sown[b] = jnp.concatenate([gather(zh, zl, occ[b, m], rmc[b]) for m in range(2)], 0)
         return 0
 
     def pair_gather(half, _):
-        fs = [gather(g[...].reshape(pairs * RF * K, NC), oc[2 * half + b], rm[2 * half + b], pairs) for b in range(2)]
-        sown[nb + half] = jnp.concatenate(fs, 0)
+        sown[nb + half] = jnp.concatenate([gather(gh, gl, oc[2 * half + b], rm[2 * half + b]) for b in range(2)], 0)
         return 0
 
     def obs_send(part, i):
@@ -441,6 +448,11 @@
             device_id_type=MESH,
         )
 
+    lax.fori_loop(0, lch, level_chunk, 0)
+    lax.fori_loop(0, nb, level_gather, 0)
+    for i in range(1, groups):
+        obs_send(1, i).start()
+
     fine_coef = coefs(1.0, 1.0, 1.0, NC)
     row_f = tile * RF - HALO
     grid_f = tiles * RF
@@ -452,19 +464,20 @@
 
         def clear(first, first_c):
             fq[j, first : first + HALO] = jnp.zeros((HALO, K, NC), F32)
-            cq[levels + j, first_c : first_c + HALO] = jnp.zeros((HALO, K, NCC), F32)
+            cq[j, first_c : first_c + HALO] = jnp.zeros((HALO, K, NCC), F32)
 
         restrict(j, 0, near, near)
         restrict(j, HALO + RF, HALO + RC, near)
         zero_edges(lambda: clear(0, 0), lambda: clear(HALO + RF, HALO + RC))
-        coarse_steps([levels + j])
+        coarse_steps(j)
 
         def put_g(i, value):
-            g[j, i] = value - doubled(cres[levels + j, i // 2])
-
-        advance([reader(fq, (j,))], [writer(ft1, ())], RF + 8, row_f, grid_f, RF, fine_coef)
-        advance([reader(ft1, ())], [writer(ft2, ())], RF + 4, row_f + 2, grid_f, RF, fine_coef)
-        advance([reader(ft2, ())], [put_g], RF, row_f + 4, grid_f, RF, fine_coef)
+            g[j, i] = value - doubled(cres[j, i // 2])
+
+        advance(reader(fq, (j,)), writer(ft1, ()), RF + 8, row_f, grid_f, RF, fine_coef)
+        advance(reader(ft1, ()), writer(ft2, ()), RF + 4, row_f + 2, grid_f, RF, fine_coef)
+        advance(reader(ft2, ()), put_g, RF, row_f + 4, grid_f, RF, fine_coef)
+        gh[j], gl[j] = halves(g[j].reshape(RF * K, NC))
 
         @pl.when(j < EARLY)
         def _():
@@ -478,37 +491,34 @@
     lax.fori_loop(0, nb // 2, pair_gather, 0)
     for i in range(1, groups):
         obs_send(0, i).start()
-
-    lax.fori_loop(0, lch, level_chunk, 0)
-    lax.fori_loop(0, nb, level_gather, 0)
-    for i in range(1, groups):
-        obs_send(1, i).start()
     sx[me] = sown[...]
-    for i in range(1, groups):
-        obs_send(0, i).wait_recv()
-        obs_send(1, i).wait_recv()
     for j in range(EARLY, pairs):
         for i in range(1, groups):
             pair_send(j, i).start()
-    for ch in range(lch):
-        for i in range(1, groups):
-            level_send(ch, i).start()
-    own_level = pltpu.make_async_copy(cres.at[pl.ds(0, levels), pl.ds(me * RQC, RQC)], za.at[me], own_sem.at[0])
+    for i in range(1, groups):
+        obs_send(1, i).wait_recv()
+    level_parts = []
+    for b in range(nb):
+        z = jnp.concatenate([sx[x, b, m * lch : (m + 1) * lch] for m in range(2) for x in range(groups)], 0)
+        z_mean = jnp.mean(z, axis=0, keepdims=True)
+        slot = iota((1, per), 1) + b * per
+        weight = jnp.where(slot < count_ref[0], 1.0 / row_of(var_ref, b * sub, sub), 0.0)
+        level_parts.append(((z - z_mean) * (1.0 / s_c), row_of(val_ref, b * sub, sub) - z_mean, weight))
+    for i in range(1, groups):
+        obs_send(0, i).wait_recv()
+    own_level = pltpu.make_async_copy(zres.at[:, pl.ds(me * RQC, RQC)], za.at[me], own_sem.at[0])
     own_pair = pltpu.make_async_copy(g.at[:, pl.ds(me * RQ, RQ)], ga.at[me], own_sem.at[1])
     own_level.start()
     own_pair.start()
 
     gram = jnp.zeros((E, E + 8), F32)
     for b in range(nb):
-        z = jnp.concatenate([sx[x, b] for x in range(groups)], 0)
+        z, rest, weight = level_parts[b]
         first = (b % 2) * pairs
         f = jnp.concatenate([sx[x, nb + b // 2, first : first + pairs] for x in range(groups)], 0)
-        z_mean = jnp.mean(z, axis=0, keepdims=True)
         f_mean = jnp.mean(f, axis=0, keepdims=True)
-        s = jnp.concatenate([(z - z_mean) * (1.0 / s_c), (f - f_mean) * (1.0 / s_f)], 0)
-        innov = row_of(val_ref, b * sub, sub) - (z_mean + f_mean)
-        slot = iota((1, per), 1) + b * per
-        weight = jnp.where(slot < count_ref[0], 1.0 / row_of(var_ref, b * sub, sub), 0.0)
+        s = jnp.concatenate([z, (f - f_mean) * (1.0 / s_f)], 0)
+        innov = rest - f_mean
         extra = jnp.where(iota((8, per), 0) == 0, weight * innov, 0.0)
         right = jnp.concatenate([s * weight, extra], 0)
         gram = gram + lax.dot_general(
@@ -526,18 +536,29 @@
             for i in range(1, groups):
                 level_send(ch, i).wait_recv()
 
-        widen = columns_out(NCC, 2)
+        p = iota((NC, NC), 0)
+        hit = level_column(p) == iota((NC, NC), 1) // 2
+        widen = [jnp.where(hit & (p % 2 == m), 1.0, 0.0).astype(BF16) for m in range(2)]
+        even = iota((K, LANES), 1) % 2 == 0
+
+        def with_other(tile):
+            other = jnp.where(even, pltpu.roll(tile, LANES - 1, axis=1), pltpu.roll(tile, 1, axis=1))
+            return tile + other
 
         def one(rc, _):
-            z = za[:, :, rc].reshape(level_all, K, NCC)
-            z_mean = jnp.mean(z, axis=0)
-            high, low = halves(((z - z_mean[None]) * (1.0 / s_c)).reshape(zk, NCC))
-            high, low = dot(high, widen).astype(BF16), dot(low, widen).astype(BF16)
-            wide_mean = select_dot(z_mean, widen)
+            z = za[:, :, rc].reshape(level_all // 2, K, NC)
+            total = jnp.sum(z, axis=0)
+            total = jnp.concatenate([with_other(total[:, v * LANES : (v + 1) * LANES]) for v in range(nv)], 1)
+            z_mean = total * (1.0 / level_all)
+            high, low = halves(((z - z_mean[None]) * (1.0 / s_c)).reshape(zk // 2, NC))
+            wide_mean = select_dot(z_mean, widen[0])
+            for m in range(2):
+                wide_high, wide_low = dot(high, widen[m]).astype(BF16), dot(low, widen[m]).astype(BF16)
+                for half in range(2):
+                    dh[2 * rc + half, m * zk // 2 : (m + 1) * zk // 2] = wide_high
+                    dl[2 * rc + half, m * zk // 2 : (m + 1) * zk // 2] = wide_low
             for half in range(2):
-                dh[2 * rc + half, 0:zk] = high
-                dl[2 * rc + half, 0:zk] = low
-                mu[2 * rc + half] = mu[2 * rc + half] + wide_mean
+                mu[2 * rc + half] = wide_mean
             return 0
 
         lax.fori_loop(0, RQC, one, 0)
@@ -557,7 +578,7 @@
         def one(r, _):
             f = ga[:, :, r].reshape(pair_all, K, NC)
             f_mean = jnp.mean(f, axis=0)
-            mu[r] = select_dot(f_mean, natural)
+            mu[r] = mu[r] + select_dot(f_mean, natural)
             anom = ((f - f_mean[None]) * (1.0 / s_f)).reshape(pair_all * K, NC)
             high = anom.astype(BF16)
             rest = anom - high.astype(F32)
@@ -587,9 +608,9 @@
             send.start()
             sends.append((send, n))
         if s == 0:
+            level_anomalies()
+        if s == len(stages) - 1:
             pair_anomalies()
-        if s == len(stages) - 1:
-            level_anomalies()
         for send, n in sends:
             send.wait_recv()
             gram = gram + ar1[n]
@@ -809,18 +830,24 @@
             pltpu.VMEM((nv, pairs * K * RF, LANES), F32),
             pltpu.VMEM((nvc, levels * K * RC, LANES), F32),
             pltpu.VMEM((pairs, RF + 2 * HALO, K, NC), F32),
-            pltpu.VMEM((levels + pairs, RC + 2 * HALO, K, NCC), F32),
+            pltpu.VMEM((pairs, RC + 2 * HALO, K, NCC), F32),
+            pltpu.VMEM((levels // 2, RC + 2 * HALO, K, NC), F32),
             pltpu.VMEM((RF + 8, K, NC), F32),
             pltpu.VMEM((RF + 4, K, NC), F32),
-            pltpu.VMEM((2, RC + 8, K, NCC), F32),
-            pltpu.VMEM((2, RC + 4, K, NCC), F32),
-            pltpu.VMEM((levels + pairs, RC, K, NCC), F32),
+            pltpu.VMEM((RC + 8, K, NCC), F32),
+            pltpu.VMEM((RC + 4, K, NCC), F32),
+            pltpu.VMEM((pairs, RC, K, NCC), F32),
+            pltpu.VMEM((levels // 2, RC, K, NC), F32),
             pltpu.VMEM((pairs, RF, K, NC), F32),
+            pltpu.VMEM((pairs, RF * K, NC), BF16),
+            pltpu.VMEM((pairs, RF * K, NC), BF16),
+            pltpu.VMEM((levels // 2, RC * K, NC), BF16),
+            pltpu.VMEM((levels // 2, RC * K, NC), BF16),
             pltpu.VMEM((groups, pairs, RQ, K, NC), F32),
-            pltpu.VMEM((groups, levels, RQC, K, NCC), F32),
+            pltpu.VMEM((groups, levels // 2, RQC, K, NC), F32),
             pltpu.VMEM((nb, NC, per), BF16),
             pltpu.VMEM((nb, RF * K, per), F32),
-            pltpu.VMEM((nb, NCC, per), BF16),
+            pltpu.VMEM((nb, 2, NC, per), BF16),
             pltpu.VMEM((nb, RC * K, per), F32),
             pltpu.VMEM((nb + nb // 2, levels, per), F32),
             pltpu.VMEM((groups, nb + nb // 2, levels, per), F32),

time: 58.4 us -> 56.5 us (0.967)
  Pallas kernels: 56.4 us -> 54.9 us
    pallas_call x1, Pallas kernels: 55 us -> 53.5 us  [per_device(): pl.pallas_call(functools.partial(cycle_kernel, sizes), out_shape=(jax.Sha...]
where the time goes in v5:
time: 56.5 us; the launch traced here: 56.2 us
  Pallas kernels  54.9 us (97%)
  between operations  1.29 us (2%)
    pallas_call x1, Pallas kernels, per_device(): pl.pallas_call(functools.partial(cycle_kernel, sizes), out_shape=(jax.Sha...  53.5 us
    pallas_call x1, Pallas kernels, per_device(): pl.pallas_call(functools.partial(order_kernel, K, RF), out_shape=(jax.Sha...  1.42 us

profile of v5, /device:TPU:0, one launch (start us, length us, event | category | flops | bytes accessed | tf_op | source)
XLA Modules:
  0.0 56.2 jit_solution(11105600342394060727)
XLA Ops:
  1.3 53.5 %cycle.1 = (f32[4,16,8,512]{3,2,1,0:T(8,128)S(1)}, f32[16,8,512]{2,1,0:T(8,128)S(1)}) custom-call(f32[512,512]{1,0:T(8,128)} %bitcast.9, f32[512,256]{1,0:T(8,128)} %bitcast.10, f32[8]{0:T(128)} %diff_in.1, f32[8]{0:T(128)} %hyper_in.1, f32[8]{0:T(128)} %drift_in.1, f32[8,128]{1,0:T(8,128)} %bitcast.11, f32[8,128]{1,0:T(8,128)} %bitcast.12, ...), custom_call_target="tpu_custom_call" | custom-call | tf_op jit(solution)/shard_map/cycle/pallas_call | solution.py:812
  54.7 1.4 %order.1 = (f32[512,512]{1,0:T(8,128)}, f32[128,512]{1,0:T(8,128)}) custom-call(f32[4,16,8,512]{3,2,1,0:T(8,128)S(1)} %get-tuple-element.6.pair_in, f32[16,8,512]{2,1,0:T(8,128)S(1)} %get-tuple-element.7.mean_in), custom_call_target="tpu_custom_call" | custom-call | tf_op jit(solution)/shard_map/order/pallas_call | solution.py:895

commit v6 on v5

--- a/solution.py
+++ b/solution.py
@@ -593,6 +593,7 @@
         lax.fori_loop(0, RQ, one, 0)
 
     slot0 = 0
+    row_sends = []
     for s, stage in enumerate(stages):
         ar0[s] = gram
         sends = []
@@ -614,8 +615,7 @@
         for send, n in sends:
             send.wait_recv()
             gram = gram + ar1[n]
-        for send, n in sends:
-            send.wait_send()
+        row_sends += [send for send, _ in sends]
         slot0 += len(sends)
 
     rows_t = E + pair_all + 8
@@ -709,6 +709,8 @@
     own_out.start()
     own_mean.start()
 
+    for send in row_sends:
+        send.wait_send()
     for way in range(2):
         for ch in range(lch):
             level_halo(ch, way).wait_send()

time: 56.5 us -> 56.5 us (level)
  no operation moved by 1% of the time
where the time goes in v6:
time: 56.5 us; the launch traced here: 56.1 us
  Pallas kernels  54.9 us (97%)
  between operations  1.29 us (2%)
    pallas_call x1, Pallas kernels, per_device(): pl.pallas_call(functools.partial(cycle_kernel, sizes), out_shape=(jax.Sha...  53.4 us
    pallas_call x1, Pallas kernels, per_device(): pl.pallas_call(functools.partial(order_kernel, K, RF), out_shape=(jax.Sha...  1.42 us

profile of v6, /device:TPU:0, one launch (start us, length us, event | category | flops | bytes accessed | tf_op | source)
XLA Modules:
  0.0 56.1 jit_solution(8916886676575822245)
XLA Ops:
  1.3 53.4 %cycle.1 = (f32[4,16,8,512]{3,2,1,0:T(8,128)S(1)}, f32[16,8,512]{2,1,0:T(8,128)S(1)}) custom-call(f32[512,512]{1,0:T(8,128)} %bitcast.9, f32[512,256]{1,0:T(8,128)} %bitcast.10, f32[8]{0:T(128)} %diff_in.1, f32[8]{0:T(128)} %hyper_in.1, f32[8]{0:T(128)} %drift_in.1, f32[8,128]{1,0:T(8,128)} %bitcast.11, f32[8,128]{1,0:T(8,128)} %bitcast.12, ...), custom_call_target="tpu_custom_call" | custom-call | tf_op jit(solution)/shard_map/cycle/pallas_call | solution.py:814
  54.7 1.4 %order.1 = (f32[512,512]{1,0:T(8,128)}, f32[128,512]{1,0:T(8,128)}) custom-call(f32[4,16,8,512]{3,2,1,0:T(8,128)S(1)} %get-tuple-element.6.pair_in, f32[16,8,512]{2,1,0:T(8,128)S(1)} %get-tuple-element.7.mean_in), custom_call_target="tpu_custom_call" | custom-call | tf_op jit(solution)/shard_map/order/pallas_call | solution.py:897
